TPU v7x, 512 devices: a whole 4x4x16 slice. The times are simulated.
512 devices in a mesh: dp: 2 (over x_lo), ctx: 32 (over x_hi, z), head: 8 (over y, core).
Axes of the slice: x: 4 (x_hi: 2, x_lo: 2; x = x_hi * 2 + x_lo), y: 4, z: 16, core: 2. Of those that a mesh axis runs over, the one named last changes fastest.
Arguments:
- queries: bfloat16 [2, 32768, 4096], P('dp', ('ctx', 'head')), may hold values from -6 to 6
- keys: bfloat16 [2, 32768, 1024], P('dp', ('ctx', 'head')), may hold values from -6 to 6
- values: bfloat16 [2, 32768, 1024], P('dp', ('ctx', 'head')), may hold values from -6 to 6
- output_gradient_stored: bfloat16 [2, 32768, 4096], P('dp', ('ctx', 'head')), may hold values from -41 to 41
Outputs:
- grad_queries: bfloat16 [2, 32768, 4096], P('dp', ('ctx', 'head'))
- key_gradient_rows: bfloat16 [2, 32768, 1024], P('dp', ('ctx', 'head'))
- value_gradient_rows: bfloat16 [2, 32768, 1024], P('dp', ('ctx', 'head'))
- grad_norm: float32 [], replicated
All inputs are finite; a program needn't handle non-finite values.
Results may differ from a plain program's by a relative error of at most 0.02.
Values may be sent and summed in bfloat16 or wider, within the bound.
No kernel may reach another device: no remote copies, remote signals or barrier semaphores. Data moves between devices by JAX's collectives and lax.ppermute only.
A program may use at most 64 MiB of HBM per device.

v0:
```python
import functools
import math

import jax
import jax.numpy as jnp
from jax import lax
from jax.experimental import pallas as pl
from jax.experimental.pallas import tpu as pltpu
from jax.sharding import PartitionSpec as P

HEAD_SIZE = 128
GROUP = 4
NEG_FILL = -1e30
SCALE = HEAD_SIZE**-0.5
LOG2E = math.log2(math.e)
NT = (((1,), (1,)), ((), ()))
NN = (((1,), (0,)), ((), ()))
TN = (((0,), (0,)), ((), ()))


def dot(a, b, dims):
    return lax.dot_general(a, b, dims, preferred_element_type=jnp.float32)


def attend_kernel(
    place, q_mine, q_theirs, g_mine, g_theirs, own, side, prev_same, prev_side,
    dq_mine, dq_theirs, own_grad, side_grad, prev_same_grad, prev_side_grad,
):
    core = place[0]
    rows = own.shape[1]
    half = rows // 2
    side_bias = jnp.where(place[1] == 1, 0.0, NEG_FILL)
    prev_bias = jnp.where(place[2] == 1, 0.0, NEG_FILL)
    biases = (None, side_bias, prev_bias, prev_bias)
    parts = (own, side, prev_same, prev_side)
    grads = (own_grad, side_grad, prev_same_grad, prev_side_grad)
    flip = core * half
    key_place = lax.broadcasted_iota(jnp.int32, (rows, rows), 0) ^ flip
    query_place = lax.broadcasted_iota(jnp.int32, (rows, rows), 1) ^ flip
    visible = key_place <= query_place
    key_sums = [None] * len(parts)
    value_sums = [None] * len(parts)
    for head in range(GROUP):
        cols = slice(head * HEAD_SIZE, (head + 1) * HEAD_SIZE)
        q = jnp.concatenate([q_mine[:, cols], q_theirs[:, cols]], axis=0)
        g = jnp.concatenate([g_mine[:, cols], g_theirs[:, cols]], axis=0)
        scores = [dot(part[0], q, NT) for part in parts]
        scores[0] = jnp.where(visible, scores[0], NEG_FILL)
        tops = [jnp.max(s, axis=0, keepdims=True) for s in scores]
        tops = [t if b is None else t + b for t, b in zip(tops, biases)]
        top = functools.reduce(jnp.maximum, tops) * (SCALE * LOG2E)
        expos = [
            jnp.exp2(s * (SCALE * LOG2E) - (top if b is None else top - b))
            for s, b in zip(scores, biases)
        ]
        total = sum(jnp.sum(e, axis=0, keepdims=True) for e in expos)
        inverse = 1.0 / total
        probs = [e * inverse for e in expos]
        dprobs = [dot(part[1], g, NT) for part in parts]
        delta = sum(jnp.sum(p * d, axis=0, keepdims=True) for p, d in zip(probs, dprobs))
        dq = None
        for i, part in enumerate(parts):
            ds = (probs[i] * (dprobs[i] - delta)).astype(jnp.bfloat16)
            low = probs[i].astype(jnp.bfloat16)
            dv = dot(low, g, NN)
            dk = dot(ds, q, NN)
            value_sums[i] = dv if head == 0 else value_sums[i] + dv
            key_sums[i] = dk if head == 0 else key_sums[i] + dk
            step = dot(ds, part[0], TN)
            dq = step if dq is None else dq + step
        dq = (dq * SCALE).astype(dq_mine.dtype)
        dq_mine[:, cols] = dq[:half]
        dq_theirs[:, cols] = dq[half:]
    for i, out in enumerate(grads):
        out[0] = (key_sums[i] * SCALE).astype(out.dtype)
        out[1] = value_sums[i].astype(out.dtype)


def attend(place, q, g, qg_theirs, own, side, prev_same, prev_side):
    rows = q.shape[0]
    wide = GROUP * HEAD_SIZE
    groups = own.shape[2] // HEAD_SIZE
    mine_spec = pl.BlockSpec((rows, wide), lambda j, p: (0, p[0] * groups + j))
    q_spec = pl.BlockSpec((rows, wide), lambda j, p: (0, j))
    g_spec = pl.BlockSpec((rows, wide), lambda j, p: (0, groups + j))
    kv_spec = pl.BlockSpec((2, own.shape[1], HEAD_SIZE), lambda j, p: (0, 0, j))
    dq_shape = jax.ShapeDtypeStruct((rows, groups * wide), q.dtype)
    return pl.pallas_call(
        attend_kernel,
        grid_spec=pltpu.PrefetchScalarGridSpec(
            num_scalar_prefetch=1,
            grid=(groups,),
            in_specs=[mine_spec, q_spec, mine_spec, g_spec] + [kv_spec] * 4,
            out_specs=[q_spec, q_spec] + [kv_spec] * 4,
        ),
        out_shape=[dq_shape, dq_shape, jax.ShapeDtypeStruct(own.shape, jnp.float32)]
        + [jax.ShapeDtypeStruct(own.shape, q.dtype)] * 3,
        compiler_params=pltpu.CompilerParams(vmem_limit_bytes=40 * 1024 * 1024),
        cost_estimate=pl.CostEstimate(
            flops=10 * 4 * own.shape[1] * 2 * rows * HEAD_SIZE * groups * GROUP,
            bytes_accessed=8 * 1024 * 1024,
            transcendentals=4 * own.shape[1] * 2 * rows * groups * GROUP,
        ),
    )(place, q, qg_theirs, g, qg_theirs, own, side, prev_same, prev_side)


def square_total(x):
    return jnp.sum(jnp.square(x.astype(jnp.float32)))


def body(queries, keys, values, output_gradient_stored):
    q, k, v, g = queries[0], keys[0], values[0], output_gradient_stored[0]
    contexts, heads = lax.axis_size("ctx"), lax.axis_size("head")
    quarter = heads // 2
    ctx, head = lax.axis_index("ctx"), lax.axis_index("head")
    core = head % 2
    is_back = head >= quarter
    place = jnp.stack(
        [core, (head // 2) % 2, jnp.where((ctx > 0) | is_back, 1, 0)]
    ).astype(jnp.int32)
    core_pairs = [(h, h ^ 1) for h in range(heads)]
    side_pairs = [(h, h ^ 2) for h in range(heads)]

    def flat(c, h):
        return c * heads + h

    chain = []
    for h in range(quarter):
        chain += [(flat(c, h), flat(c + 1, h)) for c in range(contexts - 1)]
        chain += [(flat(contexts - 1, h), flat(contexts - 1, h + quarter))]
        chain += [(flat(c, h + quarter), flat(c - 1, h + quarter)) for c in range(1, contexts)]
    back = [(target, source) for source, target in chain]

    def swap_core(x):
        return lax.ppermute(x, "head", core_pairs)

    def swap_side(x):
        return lax.ppermute(x, "head", side_pairs)

    def cut(x, which):
        width = x.shape[1] // 2
        return lax.dynamic_slice_in_dim(x, which * width, width, axis=1)

    kv_theirs = swap_core(jnp.stack([cut(k, 1 - core), cut(v, 1 - core)]))
    own = jnp.concatenate([jnp.stack([cut(k, core), cut(v, core)]), kv_theirs], axis=1)
    side = swap_side(own)
    prev_same = lax.ppermute(own, ("ctx", "head"), chain)
    qg_theirs = swap_core(jnp.concatenate([cut(q, 1 - core), cut(g, 1 - core)], axis=1))
    prev_side = lax.ppermute(side, ("ctx", "head"), chain)

    dq_mine, dq_theirs, own_grad, side_grad, prev_same_grad, prev_side_grad = attend(
        place, q, g, qg_theirs, own, side, prev_same, prev_side
    )
    next_side = lax.ppermute(prev_side_grad, ("ctx", "head"), back)
    next_same = lax.ppermute(prev_same_grad, ("ctx", "head"), back)
    dq_back = swap_core(dq_theirs)
    side_sum = (side_grad.astype(jnp.float32) + next_side.astype(jnp.float32)).astype(q.dtype)
    from_side = swap_side(side_sum)
    total = (own_grad + next_same.astype(jnp.float32) + from_side.astype(jnp.float32)).astype(
        q.dtype
    )
    rows = q.shape[0]
    total_back = swap_core(total[:, rows:])

    def join(mine, theirs):
        low = jnp.where(core == 0, mine, theirs)
        high = jnp.where(core == 0, theirs, mine)
        return jnp.concatenate([low, high], axis=-1)

    grad_kv = join(total[:, :rows], total_back)
    grad_q = join(dq_mine, dq_back)
    squares = square_total(dq_mine) + square_total(dq_theirs) + square_total(total)
    norm_square = lax.psum(squares, ("dp", "ctx", "head"))
    return (grad_q[None], grad_kv[0][None], grad_kv[1][None], jnp.sqrt(norm_square))


def solution(mesh):
    spec = P("dp", ("ctx", "head"), None)
    return jax.shard_map(
        body,
        mesh=mesh,
        in_specs=(spec, spec, spec, spec),
        out_specs=(spec, spec, spec, P()),
        check_vma=False,
    )
```

profile of v0, /device:TPU:1, one launch (start us, length us, event | category | flops | bytes accessed | tf_op | source)
XLA Modules:
  0.0 232.8 jit_solution(2473616036536680738)
XLA Ops:
  0.7 1.2 constant_dynamic-slice_fusion.2
  1.9 8.8 %collective-permute-start.1 = (bf16[2,128,512]{2,1,0:T(8,128)(2,1)S(1)}, bf16[2,128,512]{2,1,0:T(8,128)(2,1)S(1)}, u32[]{:S(2)}, u32[]{:S(2)}) collective-permute-start(bf16[2,128,512]{2,1,0:T(8,128)(2,1)S(1)} %pad_maximum_fusion.3), channel_id=1, source_target_pairs={{0,1},{1,0},{2,3},{3,2},{4,5},{5,4},{6,7},{7,6},{8,9},{9,8},{10,11... | collective-permute-start | bytes 786440 | tf_op jit(solution)/shard_map/ppermute | solution.py:135
  10.7 1.1 dynamic-slice_bitcast_fusion
  11.9 1.1 pad_maximum_fusion
  12.9 1.9 collective-permute-start
  14.9 1.9 collective-permute-start.2
  16.8 1.3 collective-permute-start.3
  18.2 11.6 %collective-permute-done.2.side = bf16[2,256,512]{2,1,0:T(8,128)(2,1)S(1)} collective-permute-done((bf16[2,256,512]{2,1,0:T(8,128)(2,1)S(1)}, bf16[2,256,512]{2,1,0:T(8,128)(2,1)S(1)}, u32[]{:S(2)}, u32[]{:S(2)}) %collective-permute-start.2) | collective-permute-done | bytes 524320 | tf_op jit(solution)/shard_map/ppermute | solution.py:138
  29.8 1.3 collective-permute-start.4
  32.8 1.0 copy-done.3
  33.8 7.4 %collective-permute-done.4.prev_side = bf16[2,256,512]{2,1,0:T(8,128)(2,1)S(1)} collective-permute-done((bf16[2,256,512]{2,1,0:T(8,128)(2,1)S(1)}, bf16[2,256,512]{2,1,0:T(8,128)(2,1)S(1)}, u32[]{:S(2)}, u32[]{:S(2)}) %collective-permute-start.4) | collective-permute-done | bytes 524320 | tf_op jit(solution)/shard_map/ppermute | solution.py:149
  42.0 1.2 copy-done.1
  43.2 1.2 copy-done.2
  44.5 1.2 copy-done.4
  45.7 1.0 copy-done.6
  46.7 1.0 copy-done.8
  47.8 1.0 copy-done.10
  48.8 21.0 %shard_map.75 = (bf16[128,2048]{1,0:T(8,128)(2,1)S(1)}, bf16[128,2048]{1,0:T(8,128)(2,1)S(1)}, f32[2,256,512]{2,1,0:T(8,128)S(1)}, bf16[2,256,512]{2,1,0:T(8,128...) custom-call(s32[3]{0:T(128)S(1)} %pad_add_fusion.place, bf16[128,4096]{1,0:T(8,128)(2,1)S(1)} %bitcast.11, ...), custom_call_target="tpu_custom_call" | custom-call | flops 5368709120 | bytes 8388608 | tf_op jit(solution)/shard_map/pallas_call | solution.py:88
  70.6 1.3 collective-permute-start.7
  71.9 1.3 collective-permute-start.6
  73.2 3.9 %collective-permute-start.5 = (bf16[128,2048]{1,0:T(8,128)(2,1)S(1)}, bf16[128,2048]{1,0:T(8,128)(2,1)S(1)}, u32[]{:S(2)}, u32[]{:S(2)}) collective-permute-start(bf16[128,2048]{1,0:T(8,128)(2,1)S(1)} %get-tuple-element.11), channel_id=1, source_target_pairs={{0,1},{1,0},{2,3},{3,2},{4,5},{5,4},{6,7},{7,6},{8,9},{9,8},{10,11... | collective-permute-start | bytes 1572872 | tf_op jit(solution)/shard_map/ppermute | solution.py:135
  77.1 0.9 multiply_reduce_fusion.1
  78.0 7.3 %collective-permute-done.7 = bf16[2,256,512]{2,1,0:T(8,128)(2,1)} collective-permute-done((bf16[2,256,512]{2,1,0:T(8,128)(2,1)}, bf16[2,256,512]{2,1,0:T(8,128)(2,1)}, u32[]{:S(2)}, u32[]{:S(2)}) %collective-permute-start.7) | collective-permute-done | bytes 524320 | tf_op jit(solution)/shard_map/ppermute | solution.py:154
  85.3 2.0 add_convert_fusion.1
  87.3 3.0 %collective-permute-start.8 = (bf16[2,256,512]{2,1,0:T(8,128)(2,1)}, bf16[2,256,512]{2,1,0:T(8,128)(2,1)}, u32[]{:S(2)}, u32[]{:S(2)}) collective-permute-start(bf16[2,256,512]{2,1,0:T(8,128)(2,1)} %add_convert_fusion.1), channel_id=1, source_target_pairs={{0,2},{1,3},{2,0},{3,1},{4,6},{5,7},{6,4},{7,5},{8,10},{9,11},{10,... | collective-permute-start | bytes 1572872 | tf_op jit(solution)/shard_map/ppermute | solution.py:138
  90.2 0.9 multiply_reduce_fusion.2
  92.5 4.0 %collective-permute-done.6 = bf16[2,256,512]{2,1,0:T(8,128)(2,1)} collective-permute-done((bf16[2,256,512]{2,1,0:T(8,128)(2,1)}, bf16[2,256,512]{2,1,0:T(8,128)(2,1)}, u32[]{:S(2)}, u32[]{:S(2)}) %collective-permute-start.6) | collective-permute-done | bytes 524320 | tf_op jit(solution)/shard_map/ppermute | solution.py:155
  96.5 1.5 collective-permute-done.8
  98.0 2.1 multiply_reduce_fusion
  100.1 7.7 %collective-permute-start.9 = (bf16[2,128,512]{2,1,0:T(8,128)(2,1)S(1)}, bf16[2,128,512]{2,1,0:T(8,128)(2,1)S(1)}, u32[]{:S(2)}, u32[]{:S(2)}) collective-permute-start(bf16[2,128,512]{2,1,0:T(8,128)(2,1)S(1)} %slice.17), channel_id=1, source_target_pairs={{0,1},{1,0},{2,3},{3,2},{4,5},{5,4},{6,7},{7,6},{8,9},{9,8},{10,11... | collective-permute-start | bytes 786440 | tf_op jit(solution)/shard_map/ppermute | solution.py:135
  108.5 1.0 maximum_bitcast_fusion
  109.5 120.6 %psum.7 = f32[]{:T(128)} all-reduce(f32[]{:T(128)S(6)} %add.46), channel_id=1, replica_groups=mesh['dp'=2,'ctx'=32,'head'=8] {'dp','ctx','head'}, use_global_device_ids=true, to_apply=%region_3.4 | all-reduce | flops 1 | bytes 8 | tf_op jit(solution)/shard_map/psum | solution.py:173
  (29 shorter events, 4.4 us)
Async XLA Ops:
  0.6 10.1 %copy-start = (bf16[1,128,4096]{2,1,0:T(8,128)(2,1)S(1)}, bf16[1,128,4096]{2,1,0:T(8,128)(2,1)}, u32[]{:S(2)}) copy-start(bf16[1,128,4096]{2,1,0:T(8,128)(2,1)} %param.4) | copy-start | bytes 3145732
  1.9 12.9 %collective-permute-start.1 = (bf16[2,128,512]{2,1,0:T(8,128)(2,1)S(1)}, bf16[2,128,512]{2,1,0:T(8,128)(2,1)S(1)}, u32[]{:S(2)}, u32[]{:S(2)}) collective-permute-start(bf16[2,128,512]{2,1,0:T(8,128)(2,1)S(1)} %pad_maximum_fusion.3), channel_id=1, source_target_pairs={{0,1},{1,0},{2,3},{3,2},{4,5},{5,4},{6,7},{7,6},{8,9},{9,8},{10,11... | collective-permute-start | bytes 786440 | tf_op jit(solution)/shard_map/ppermute | solution.py:135
  12.9 19.9 %collective-permute-start = (bf16[128,4096]{1,0:T(8,128)(2,1)}, bf16[128,4096]{1,0:T(8,128)(2,1)S(1)}, u32[]{:S(2)}, u32[]{:S(2)}) collective-permute-start(bf16[128,4096]{1,0:T(8,128)(2,1)} %pad_maximum_fusion), channel_id=1, source_target_pairs={{0,1},{1,0},{2,3},{3,2},{4,5},{5,4},{6,7},{7,6},{8,9},{9,8},{10,11... | collective-permute-start | bytes 3145736 | tf_op jit(solution)/shard_map/ppermute | solution.py:135
  14.9 14.9 %collective-permute-start.2 = (bf16[2,256,512]{2,1,0:T(8,128)(2,1)S(1)}, bf16[2,256,512]{2,1,0:T(8,128)(2,1)S(1)}, u32[]{:S(2)}, u32[]{:S(2)}) collective-permute-start(bf16[2,256,512]{2,1,0:T(8,128)(2,1)S(1)} %pad_maximum_fusion.1.own), channel_id=1, source_target_pairs={{0,2},{1,3},{2,0},{3,1},{4,6},{5,7},{6,4},{7,5},{8,10},{9,11},{10,... | collective-permute-start | bytes 1572872 | tf_op jit(solution)/shard_map/ppermute | solution.py:138
  16.8 15.1 %collective-permute-start.3 = (bf16[2,256,512]{2,1,0:T(8,128)(2,1)S(1)}, bf16[2,256,512]{2,1,0:T(8,128)(2,1)S(1)}, u32[]{:S(2)}, u32[]{:S(2)}) collective-permute-start(bf16[2,256,512]{2,1,0:T(8,128)(2,1)S(1)} %pad_maximum_fusion.1.own), channel_id=1, source_target_pairs={{0,8},{8,16},{16,24},{24,32},{32,40},{40,48},{48,56},{56,64},{64,7... | collective-permute-start | bytes 1572872 | tf_op jit(solution)/shard_map/ppermute | solution.py:147
  29.8 11.4 %collective-permute-start.4 = (bf16[2,256,512]{2,1,0:T(8,128)(2,1)S(1)}, bf16[2,256,512]{2,1,0:T(8,128)(2,1)S(1)}, u32[]{:S(2)}, u32[]{:S(2)}) collective-permute-start(bf16[2,256,512]{2,1,0:T(8,128)(2,1)S(1)} %collective-permute-done.2.side), channel_id=1, source_target_pairs={{0,8},{8,16},{16,24},{24,32},{32,40},{40,48},{48,56},{56,64},{64,7... | collective-permute-start | bytes 1572872 | tf_op jit(solution)/shard_map/ppermute | solution.py:149
  31.1 0.8 copy-start.5
  32.0 0.8 copy-start.7
  32.8 1.0 copy-start.3
  41.2 0.8 copy-start.9
  42.0 1.2 copy-start.1
  43.2 1.2 copy-start.2
  44.5 1.2 copy-start.4
  45.7 1.0 copy-start.6
  46.7 1.0 copy-start.8
  47.8 1.0 copy-start.10
  69.8 0.8 copy-start.11
  70.6 14.6 %collective-permute-start.7 = (bf16[2,256,512]{2,1,0:T(8,128)(2,1)}, bf16[2,256,512]{2,1,0:T(8,128)(2,1)}, u32[]{:S(2)}, u32[]{:S(2)}) collective-permute-start(bf16[2,256,512]{2,1,0:T(8,128)(2,1)} %get-tuple-element.15), channel_id=1, source_target_pairs={{8,0},{16,8},{24,16},{32,24},{40,32},{48,40},{56,48},{64,56},{72,6... | collective-permute-start | bytes 1572872 | tf_op jit(solution)/shard_map/ppermute | solution.py:154
  71.9 24.6 %collective-permute-start.6 = (bf16[2,256,512]{2,1,0:T(8,128)(2,1)}, bf16[2,256,512]{2,1,0:T(8,128)(2,1)}, u32[]{:S(2)}, u32[]{:S(2)}) collective-permute-start(bf16[2,256,512]{2,1,0:T(8,128)(2,1)} %copy-done.11), channel_id=1, source_target_pairs={{8,0},{16,8},{24,16},{32,24},{40,32},{48,40},{56,48},{64,56},{72,6... | collective-permute-start | bytes 1572872 | tf_op jit(solution)/shard_map/ppermute | solution.py:155
  73.2 19.2 %collective-permute-start.5 = (bf16[128,2048]{1,0:T(8,128)(2,1)S(1)}, bf16[128,2048]{1,0:T(8,128)(2,1)S(1)}, u32[]{:S(2)}, u32[]{:S(2)}) collective-permute-start(bf16[128,2048]{1,0:T(8,128)(2,1)S(1)} %get-tuple-element.11), channel_id=1, source_target_pairs={{0,1},{1,0},{2,3},{3,2},{4,5},{5,4},{6,7},{7,6},{8,9},{9,8},{10,11... | collective-permute-start | bytes 1572872 | tf_op jit(solution)/shard_map/ppermute | solution.py:135
  87.3 10.7 %collective-permute-start.8 = (bf16[2,256,512]{2,1,0:T(8,128)(2,1)}, bf16[2,256,512]{2,1,0:T(8,128)(2,1)}, u32[]{:S(2)}, u32[]{:S(2)}) collective-permute-start(bf16[2,256,512]{2,1,0:T(8,128)(2,1)} %add_convert_fusion.1), channel_id=1, source_target_pairs={{0,2},{1,3},{2,0},{3,1},{4,6},{5,7},{6,4},{7,5},{8,10},{9,11},{10,... | collective-permute-start | bytes 1572872 | tf_op jit(solution)/shard_map/ppermute | solution.py:138
  100.1 130.7 %collective-permute-start.9 = (bf16[2,128,512]{2,1,0:T(8,128)(2,1)S(1)}, bf16[2,128,512]{2,1,0:T(8,128)(2,1)S(1)}, u32[]{:S(2)}, u32[]{:S(2)}) collective-permute-start(bf16[2,128,512]{2,1,0:T(8,128)(2,1)S(1)} %slice.17), channel_id=1, source_target_pairs={{0,1},{1,0},{2,3},{3,2},{4,5},{5,4},{6,7},{7,6},{8,9},{9,8},{10,11... | collective-permute-start | bytes 786440 | tf_op jit(solution)/shard_map/ppermute | solution.py:135
where the time goes:
time: 234 us; the launch traced here: 233 us
  blocking collectives  121 us (52%)
  starting transfers between devices  32.4 us (14%)
  waiting for transfers between devices  31.9 us (14%)
  Pallas kernels  21 us (9%)
  local copies, waits for them, and re-layouts  13.3 us (6%)
  other arithmetic  9.01 us (4%)
  between operations  4.63 us (2%)
    psum x1, blocking collectives, body(): norm_square = lax.psum(squares, ('dp', 'ctx', 'head'))  121 us
    ppermute x4, starting transfers between devices, swap_core(): return lax.ppermute(x, 'head', core_pairs)  22.3 us
    pallas_call x1, Pallas kernels, attend(): pl.pallas_call(attend_kernel, grid_spec=pltpu.PrefetchScalarGridSpec(num_...  21 us
    ppermute x2, waiting for transfers between devices, swap_side(): return lax.ppermute(x, 'head', side_pairs)  13.1 us
    unnamed x24, local copies, waits for them, and re-layouts  11 us
    ppermute x1, waiting for transfers between devices, body(): prev_side = lax.ppermute(side, ('ctx', 'head'), chain)  7.44 us
    ppermute x1, waiting for transfers between devices, body(): next_side = lax.ppermute(prev_side_grad, ('ctx', 'head'), back)  7.28 us
    ppermute x2, starting transfers between devices, swap_side(): return lax.ppermute(x, 'head', side_pairs)  4.88 us
  transfers between devices with their start and end apart: 10, of which 5 were waited for; matrix products, arithmetic and copies ran while one was open for 3% of the time, Pallas kernels for 0%

commit v1 on v0

v1 whole, which is shorter than its diff:
```python
import functools
import math

import jax
import jax.numpy as jnp
from jax import lax
from jax.experimental import pallas as pl
from jax.experimental.pallas import tpu as pltpu
from jax.sharding import PartitionSpec as P

HEAD_SIZE = 128
GROUP = 4
NEG_FILL = -1e30
SCALE = HEAD_SIZE**-0.5
RATE = SCALE * math.log2(math.e)
VMEM = 60 * 1024 * 1024
NT = (((1,), (1,)), ((), ()))
NN = (((1,), (0,)), ((), ()))
TN = (((0,), (0,)), ((), ()))


def dot(a, b, dims):
    return lax.dot_general(a, b, dims, preferred_element_type=jnp.float32)


def pair(mine, theirs, head):
    cols = slice(head * HEAD_SIZE, (head + 1) * HEAD_SIZE)
    return jnp.concatenate([mine[:, cols], theirs[:, cols]], axis=0)


def own_scores(place, keys, q):
    rows = keys.shape[0]
    flip = place[0] * (rows // 2)
    key_place = lax.broadcasted_iota(jnp.int32, (rows, rows), 0) ^ flip
    query_place = lax.broadcasted_iota(jnp.int32, (rows, rows), 1) ^ flip
    return jnp.where(key_place <= query_place, dot(keys, q, NT), NEG_FILL)


def own_kernel(place, q_mine, q_theirs, g_mine, g_theirs, own, stats):
    for head in range(GROUP):
        q = pair(q_mine, q_theirs, head)
        g = pair(g_mine, g_theirs, head)
        scores = own_scores(place, own[0], q)
        top = jnp.max(scores, axis=0, keepdims=True)
        expos = jnp.exp2(scores * RATE - top * RATE)
        dprobs = dot(own[1], g, NT)
        stats[0, head : head + 1] = top
        stats[0, GROUP + head : GROUP + head + 1] = jnp.sum(expos, axis=0, keepdims=True)
        stats[0, 2 * GROUP + head : 2 * GROUP + head + 1] = jnp.sum(
            expos * dprobs, axis=0, keepdims=True
        )


def remote_kernel(
    place, q_mine, q_theirs, g_mine, g_theirs, own_stats, cross, same, side,
    side_grad, same_grad, cross_grad, dscores, stats,
):
    side_bias = jnp.where(place[1] == 1, 0.0, NEG_FILL)
    prev_bias = jnp.where(place[2] == 1, 0.0, NEG_FILL)
    biases = (side_bias, prev_bias, prev_bias)
    parts = (side, same, cross)
    rows = side.shape[1]
    key_sums = [None] * len(parts)
    value_sums = [None] * len(parts)
    for head in range(GROUP):
        q = pair(q_mine, q_theirs, head)
        g = pair(g_mine, g_theirs, head)
        own_top = own_stats[0, head : head + 1]
        own_total = own_stats[0, GROUP + head : GROUP + head + 1]
        own_delta = own_stats[0, 2 * GROUP + head : 2 * GROUP + head + 1]
        scores = [dot(part[0], q, NT) for part in parts]
        tops = [jnp.max(s, axis=0, keepdims=True) + b for s, b in zip(scores, biases)]
        top = functools.reduce(jnp.maximum, tops + [own_top]) * RATE
        expos = [jnp.exp2(s * RATE - (top - b)) for s, b in zip(scores, biases)]
        weight = jnp.exp2(own_top * RATE - top)
        total = sum(jnp.sum(e, axis=0, keepdims=True) for e in expos) + own_total * weight
        inverse = 1.0 / total
        dprobs = [dot(part[1], g, NT) for part in parts]
        delta = sum(jnp.sum(e * d, axis=0, keepdims=True) for e, d in zip(expos, dprobs))
        delta = (delta + own_delta * weight) * inverse
        stats[0, head : head + 1] = top
        stats[0, GROUP + head : GROUP + head + 1] = inverse
        stats[0, 2 * GROUP + head : 2 * GROUP + head + 1] = delta
        for i in range(len(parts)):
            probs = expos[i] * inverse
            low = probs.astype(jnp.bfloat16)
            ds = (probs * (dprobs[i] - delta)).astype(jnp.bfloat16)
            dscores[0, head, i * rows : (i + 1) * rows] = ds
            dv = dot(low, g, NN)
            dk = dot(ds, q, NN)
            value_sums[i] = dv if head == 0 else value_sums[i] + dv
            key_sums[i] = dk if head == 0 else key_sums[i] + dk
    for i, out in enumerate((side_grad, same_grad, cross_grad)):
        out[0] = (key_sums[i] * SCALE).astype(out.dtype)
        out[1] = value_sums[i].astype(out.dtype)


def rest_kernel(
    place, q_mine, q_theirs, g_mine, g_theirs, stats, own, side, same, cross, dscores,
    dq_mine, dq_theirs, own_grad, squares,
):
    half = dq_mine.shape[0]
    rows = 2 * half
    key_sum = value_sum = None
    square = jnp.zeros((8, HEAD_SIZE), jnp.float32)
    for head in range(GROUP):
        q = pair(q_mine, q_theirs, head)
        g = pair(g_mine, g_theirs, head)
        top = stats[0, head : head + 1]
        inverse = stats[0, GROUP + head : GROUP + head + 1]
        delta = stats[0, 2 * GROUP + head : 2 * GROUP + head + 1]
        probs = jnp.exp2(own_scores(place, own[0], q) * RATE - top) * inverse
        low = probs.astype(jnp.bfloat16)
        ds = (probs * (dot(own[1], g, NT) - delta)).astype(jnp.bfloat16)
        dv = dot(low, g, NN)
        dk = dot(ds, q, NN)
        value_sum = dv if head == 0 else value_sum + dv
        key_sum = dk if head == 0 else key_sum + dk
        dq = dot(ds, own[0], TN)
        for i, part in enumerate((side, same, cross)):
            dq = dq + dot(dscores[0, head, i * rows : (i + 1) * rows], part[0], TN)
        dq = (dq * SCALE).astype(dq_mine.dtype)
        cols = slice(head * HEAD_SIZE, (head + 1) * HEAD_SIZE)
        dq_mine[:, cols] = dq[:half]
        dq_theirs[:, cols] = dq[half:]
        wide = dq.astype(jnp.float32)
        square = square + jnp.sum((wide * wide).reshape(rows // 8, 8, HEAD_SIZE), axis=0)
    own_grad[0] = key_sum * SCALE
    own_grad[1] = value_sum

    @pl.when(pl.program_id(0) == 0)
    def _():
        squares[...] = jnp.zeros_like(squares)

    squares[...] += square


def total_kernel(own, side, same, cross, dq_squares, mine, theirs, sums):
    total = own[...] + side[...].astype(jnp.float32)
    total = total + same[...].astype(jnp.float32) + cross[...].astype(jnp.float32)
    total = total.astype(mine.dtype)
    half = mine.shape[1]
    mine[...] = total[:, :half]
    theirs[...] = total[:, half:]
    wide = total.astype(jnp.float32)
    square = jnp.sum((wide * wide).reshape(-1, 8, wide.shape[-1]), axis=0)
    square = jnp.sum(square, keepdims=True) + jnp.sum(dq_squares[...], keepdims=True)
    sums[...] = jnp.broadcast_to(square, sums.shape)


def call(kernel, groups, ins, outs, flops, exps, *args):
    return pl.pallas_call(
        kernel,
        grid_spec=pltpu.PrefetchScalarGridSpec(
            num_scalar_prefetch=1,
            grid=(groups,),
            in_specs=ins,
            out_specs=[spec for spec, _ in outs],
        ),
        out_shape=[shape for _, shape in outs],
        compiler_params=pltpu.CompilerParams(vmem_limit_bytes=VMEM),
        cost_estimate=pl.CostEstimate(
            flops=flops, bytes_accessed=4 * 1024 * 1024, transcendentals=exps
        ),
    )(*args)


def all_sum(x, axes):
    given = lax.all_to_all(x, axes, 0, 0, tiled=True)
    return jnp.sum(given, axis=0, keepdims=True)


def body(queries, keys, values, output_gradient_stored):
    q, k, v, g = queries[0], keys[0], values[0], output_gradient_stored[0]
    contexts, heads = lax.axis_size("ctx"), lax.axis_size("head")
    quarter = heads // 2
    ctx, head = lax.axis_index("ctx"), lax.axis_index("head")
    core = head % 2
    is_back = head >= quarter
    place = jnp.stack(
        [core, (head // 2) % 2, jnp.where((ctx > 0) | is_back, 1, 0)]
    ).astype(jnp.int32)
    core_pairs = [(h, h ^ 1) for h in range(heads)]
    side_pairs = [(h, h ^ 2) for h in range(heads) if h & 2 == 0]
    side_back = [(target, source) for source, target in side_pairs]

    def flat(c, h):
        return c * heads + h

    chain = []
    for h in range(quarter):
        chain += [(flat(c, h), flat(c + 1, h)) for c in range(contexts - 1)]
        chain += [(flat(contexts - 1, h), flat(contexts - 1, h + quarter))]
        chain += [(flat(c, h + quarter), flat(c - 1, h + quarter)) for c in range(1, contexts)]
    slant = [(source, target ^ 2) for source, target in chain]
    chain_back = [(target, source) for source, target in chain]
    slant_back = [(target, source) for source, target in slant]
    both = ("ctx", "head")

    def swap_core(x):
        return lax.ppermute(x, "head", core_pairs)

    def cut(x, which):
        width = x.shape[1] // 2
        return lax.dynamic_slice_in_dim(x, which * width, width, axis=1)

    rows = q.shape[0]
    kv_theirs = swap_core(jnp.stack([cut(k, 1 - core), cut(v, 1 - core)]))
    own = jnp.concatenate([jnp.stack([cut(k, core), cut(v, core)]), kv_theirs], axis=1)
    side = lax.ppermute(own, "head", side_pairs)
    same = lax.ppermute(own, both, chain)
    cross = lax.ppermute(own, both, slant)
    qg_theirs = jnp.concatenate([cut(q, 1 - core), cut(g, 1 - core)], axis=1)
    qg_theirs, own_late = lax.optimization_barrier((qg_theirs, own))
    qg_theirs = swap_core(qg_theirs)

    groups = own.shape[2] // HEAD_SIZE
    wide = GROUP * HEAD_SIZE
    span = own.shape[1]
    mine_spec = pl.BlockSpec((rows, wide), lambda j, p: (0, p[0] * groups + j))
    q_spec = pl.BlockSpec((rows, wide), lambda j, p: (0, j))
    g_spec = pl.BlockSpec((rows, wide), lambda j, p: (0, groups + j))
    kv_spec = pl.BlockSpec((2, span, HEAD_SIZE), lambda j, p: (0, 0, j))
    k_spec = pl.BlockSpec((1, span, HEAD_SIZE), lambda j, p: (0, 0, j))
    stat_spec = pl.BlockSpec((1, 4 * GROUP, span), lambda j, p: (j, 0, 0))
    ds_spec = pl.BlockSpec((1, GROUP, 3 * span, span), lambda j, p: (j, 0, 0, 0))
    square_spec = pl.BlockSpec((8, HEAD_SIZE), lambda j, p: (0, 0))
    qg_specs = [mine_spec, q_spec, mine_spec, g_spec]
    stat = (stat_spec, jax.ShapeDtypeStruct((groups, 4 * GROUP, span), jnp.float32))
    grad = (kv_spec, jax.ShapeDtypeStruct(own.shape, q.dtype))
    part = (q_spec, jax.ShapeDtypeStruct((rows, groups * wide), q.dtype))
    unit = 2 * span * span * HEAD_SIZE * groups * GROUP
    exps = span * span * groups * GROUP
    rows_in = (place, q, qg_theirs, g, qg_theirs)

    (own_stats,) = call(
        own_kernel, groups, qg_specs + [kv_spec], [stat], 2 * unit, exps, *rows_in, own
    )
    side_grad, same_grad, cross_grad, dscores, stats = call(
        remote_kernel,
        groups,
        qg_specs + [stat_spec] + [kv_spec] * 3,
        [grad] * 3
        + [(ds_spec, jax.ShapeDtypeStruct((groups, GROUP, 3 * span, span), q.dtype)), stat],
        12 * unit,
        3 * exps,
        *rows_in, own_stats, cross, same, side,
    )
    from_side = lax.ppermute(side_grad, "head", side_back)
    next_same = lax.ppermute(same_grad, both, chain_back)
    next_cross = lax.ppermute(cross_grad, both, slant_back)
    dq_mine, dq_theirs, own_grad, dq_squares = call(
        rest_kernel,
        groups,
        qg_specs + [stat_spec, kv_spec] + [k_spec] * 3 + [ds_spec],
        [part, part, (kv_spec, jax.ShapeDtypeStruct(own.shape, jnp.float32))]
        + [(square_spec, jax.ShapeDtypeStruct((8, HEAD_SIZE), jnp.float32))],
        8 * unit,
        exps,
        *rows_in, stats, own, side, same, cross, dscores,
    )
    dq_back = swap_core(dq_theirs)
    near = lax.axis_size("head")
    half_shape = jax.ShapeDtypeStruct((2, rows, own.shape[2]), q.dtype)
    total_mine, total_theirs, sums = pl.pallas_call(
        total_kernel,
        out_shape=[half_shape, half_shape, jax.ShapeDtypeStruct((near, HEAD_SIZE), jnp.float32)],
        compiler_params=pltpu.CompilerParams(vmem_limit_bytes=24 * 1024 * 1024),
    )(own_grad, from_side, next_same, next_cross, dq_squares)

    def join(mine, theirs):
        low = jnp.where(core == 0, mine, theirs)
        high = jnp.where(core == 0, theirs, mine)
        return jnp.concatenate([low, high], axis=-1)

    grad_q = join(dq_mine, dq_back)
    sums = all_sum(sums, "head")
    grad_kv = join(total_mine, swap_core(total_theirs))
    norm_square = all_sum(jnp.broadcast_to(sums, (2 * contexts, HEAD_SIZE)), ("dp", "ctx"))[0, 0]
    return (grad_q[None], grad_kv[0][None], grad_kv[1][None], jnp.sqrt(norm_square))


def solution(mesh):
    spec = P("dp", ("ctx", "head"), None)
    return jax.shard_map(
        body,
        mesh=mesh,
        in_specs=(spec, spec, spec, spec),
        out_specs=(spec, spec, spec, P()),
        check_vma=False,
    )
```

time: 234 us -> 143 us (0.61)
  blocking collectives: 121 us -> 0 us
  starting transfers between devices: 32.4 us -> 60.1 us
  Pallas kernels: 21 us -> 33.6 us
  local copies, waits for them, and re-layouts: 13.3 us -> 5.97 us
  other arithmetic: 9.01 us -> 2.79 us
  waiting for transfers between devices: 31.9 us -> 38.1 us
  between operations: 4.63 us -> 2.09 us
    psum x1 -> x0, blocking collectives: 121 us -> none  [body(): norm_square = lax.psum(squares, ('dp', 'ctx', 'head'))]
    all_to_all x0 -> x2, starting transfers between devices: none -> 35.1 us  [all_sum(): given = lax.all_to_all(x, axes, 0, 0, tiled=True)]
    all_to_all x0 -> x2, waiting for transfers between devices: none -> 14.6 us  [all_sum(): given = lax.all_to_all(x, axes, 0, 0, tiled=True)]
    pallas_call x1 -> x4, Pallas kernels: 21 us -> 33.6 us  [the longest x3 32.3 us: call(): pl.pallas_call(kernel, grid_spec=pltpu.PrefetchScalarGridSpec(num_scalar_...]
    ppermute x6, waiting for transfers between devices: 31.9 us -> 23.5 us  [the longest x1 11.2 us: body(): cross = lax.ppermute(own, both, slant)]
    unnamed x24 -> x12, local copies, waits for them, and re-layouts: 11 us -> 2.89 us
    ppermute x4, starting transfers between devices: 22.3 us -> 15.6 us  [swap_core(): return lax.ppermute(x, 'head', core_pairs)]
    reduce_sum x3 -> x2, other arithmetic: 3.84 us -> 0.05 us  [all_sum(): return jnp.sum(given, axis=0, keepdims=True)]
  transfers between devices with their start and end apart: 10 -> 12, of which waited for: 5 -> 5; matrix products, arithmetic and copies ran while one was open for 3% -> 3% of each run, Pallas kernels for 0% -> 12%
where the time goes in v1:
time: 143 us
  starting transfers between devices  60.1 us (42%)
  waiting for transfers between devices  38.1 us (27%)
  Pallas kernels  33.6 us (23%)
  local copies, waits for them, and re-layouts  5.97 us (4%)
  other arithmetic  2.79 us (2%)
  between operations  2.09 us (1%)
    all_to_all x2, starting transfers between devices, all_sum(): given = lax.all_to_all(x, axes, 0, 0, tiled=True)  35.1 us
    pallas_call x3, Pallas kernels, call(): pl.pallas_call(kernel, grid_spec=pltpu.PrefetchScalarGridSpec(num_scalar_...  32.3 us
    ppermute x4, starting transfers between devices, swap_core(): return lax.ppermute(x, 'head', core_pairs)  15.6 us
    all_to_all x2, waiting for transfers between devices, all_sum(): given = lax.all_to_all(x, axes, 0, 0, tiled=True)  14.6 us
    ppermute x1, waiting for transfers between devices, body(): cross = lax.ppermute(own, both, slant)  11.2 us
    ppermute x1, waiting for transfers between devices, body(): next_cross = lax.ppermute(cross_grad, both, slant_back)  11.1 us
    unnamed x12, local copies, waits for them, and re-layouts  2.89 us
  transfers between devices with their start and end apart: 12, of which 5 were waited for; matrix products, arithmetic and copies ran while one was open for 3% of the time, Pallas kernels for 12%

profile of v1, /device:TPU:1, one launch (start us, length us, event | category | flops | bytes accessed | tf_op | source)
XLA Modules:
  0.0 142.7 jit_solution(15268658237657334586)
XLA Ops:
  0.7 1.1 constant_dynamic-slice_fusion.2
  1.8 8.8 %collective-permute-start = (bf16[2,128,512]{2,1,0:T(8,128)(2,1)S(1)}, bf16[2,128,512]{2,1,0:T(8,128)(2,1)S(1)}, u32[]{:S(2)}, u32[]{:S(2)}) collective-permute-start(bf16[2,128,512]{2,1,0:T(8,128)(2,1)S(1)} %pad_maximum_fusion.3), channel_id=1, source_target_pairs={{0,1},{1,0},{2,3},{3,2},{4,5},{5,4},{6,7},{7,6},{8,9},{9,8},{10,11... | collective-permute-start | bytes 786440 | tf_op jit(solution)/shard_map/ppermute | solution.py:201
  10.6 1.3 dynamic-slice_bitcast_fusion
  11.9 0.1 pad_maximum_fusion
  12.1 2.0 %collective-permute-start.1 = (bf16[128,4096]{1,0:T(8,128)(2,1)S(1)}, bf16[128,4096]{1,0:T(8,128)(2,1)S(1)}, u32[]{:S(2)}, u32[]{:S(2)}) collective-permute-start(bf16[128,4096]{1,0:T(8,128)(2,1)S(1)} %pad_maximum_fusion), channel_id=1, source_target_pairs={{0,1},{1,0},{2,3},{3,2},{4,5},{5,4},{6,7},{7,6},{8,9},{9,8},{10,11... | collective-permute-start | bytes 3145736 | tf_op jit(solution)/shard_map/ppermute | solution.py:201
  14.1 1.3 collective-permute-start.4
  15.4 2.1 %collective-permute-start.3 = (bf16[2,256,512]{2,1,0:T(8,128)(2,1)S(1)}, bf16[2,256,512]{2,1,0:T(8,128)(2,1)}, u32[]{:S(2)}, u32[]{:S(2)}) collective-permute-start(bf16[2,256,512]{2,1,0:T(8,128)(2,1)S(1)} %pad_maximum_fusion.1.own), channel_id=1, source_target_pairs={{0,8},{8,16},{16,24},{24,32},{32,40},{40,48},{48,56},{56,64},{64,7... | collective-permute-start | bytes 1572872 | tf_op jit(solution)/shard_map/ppermute | solution.py:211
  17.5 2.1 %collective-permute-start.2 = (bf16[2,256,512]{2,1,0:T(8,128)(2,1)S(1)}, bf16[2,256,512]{2,1,0:T(8,128)(2,1)}, u32[]{:S(2)}, u32[]{:S(2)}) collective-permute-start(bf16[2,256,512]{2,1,0:T(8,128)(2,1)S(1)} %pad_maximum_fusion.1.own), channel_id=1, source_target_pairs={{0,10},{8,18},{16,26},{24,34},{32,42},{40,50},{48,58},{56,66},{64,... | collective-permute-start | bytes 1572872 | tf_op jit(solution)/shard_map/ppermute | solution.py:212
  19.6 0.6 pad_add_fusion.place
  20.2 1.0 copy-done.2
  21.2 5.6 %shard_map.75.own_stats = f32[4,16,256]{2,1,0:T(8,128)} custom-call(s32[3]{0:T(128)} %pad_add_fusion.place, bf16[128,4096]{1,0:T(8,128)(2,1)} %bitcast.18, bf16[128,4096]{1,0:T(8,128)(2,1)} %copy-done.2, bf16[128,4096]{1,0:T(8,128)(2,1)} %bitcast.21, bf16[128,4096]{1,0:T(8,128)(2,1)} %copy-done.2, bf16[2,256,512]{2,1,0:T(8,128)(2,1)} %copy-done.3), custom_call_target="tpu_custom_call" | custom-call | flops 536870912 | bytes 4194304 | tf_op jit(solution)/shard_map/pallas_call | solution.py:152
  26.8 1.2 collective-permute-done.3.same
  27.9 11.2 %collective-permute-done.2.cross = bf16[2,256,512]{2,1,0:T(8,128)(2,1)} collective-permute-done((bf16[2,256,512]{2,1,0:T(8,128)(2,1)S(1)}, bf16[2,256,512]{2,1,0:T(8,128)(2,1)}, u32[]{:S(2)}, u32[]{:S(2)}) %collective-permute-start.2) | collective-permute-done | bytes 524320 | tf_op jit(solution)/shard_map/ppermute | solution.py:212
  39.2 16.0 %shard_map.76 = (bf16[2,256,512]{2,1,0:T(8,128)(2,1)}, bf16[2,256,512]{2,1,0:T(8,128)(2,1)}, bf16[2,256,512]{2,1,0:T(8,128)(2,1)}, bf16[4,4,768,256]{3,2,1,0:T(8,128)(2,1)}, f32[4,16,256]{2,1,0:T(8,128)}) custom-call(s32[3]{0:T(128)} %pad_add_fusion.place, bf16[128,4096]{1,0:T(8,128)(2,1)} %bitcast.19, bf16[128,4096]{1,0:T(8,128)(2,1)} %copy-done.2, ...), custom_call_target="tpu_custom_call" | custom-call | flops 3221225472 | bytes 4194304 | tf_op jit(solution)/shard_map/pallas_call | solution.py:152
  55.1 1.3 collective-permute-start.6
  56.4 1.3 collective-permute-start.7
  57.7 1.3 collective-permute-start.8
  59.0 10.8 %shard_map.77 = (bf16[128,2048]{1,0:T(8,128)(2,1)}, bf16[128,2048]{1,0:T(8,128)(2,1)}, f32[2,256,512]{2,1,0:T(8,128)}, f32[8,128]{1,0:T(8,128)}) custom-call(s32[3]{0:T(128)} %pad_add_fusion.place, bf16[128,4096]{1,0:T(8,128)(2,1)} %bitcast.20, bf16[128,4096]{1,0:T(8,128)(2,1)} %copy-done.2, bf16[128,4096]{1,0:T(8,128)(2,1)} %bitcast.23, ...), custom_call_target="tpu_custom_call" | custom-call | flops 2147483648 | bytes 4194304 | tf_op jit(solution)/shard_map/pallas_call | solution.py:152
  69.9 2.8 %collective-permute-start.5 = (bf16[128,2048]{1,0:T(8,128)(2,1)}, bf16[128,2048]{1,0:T(8,128)(2,1)S(1)}, u32[]{:S(2)}, u32[]{:S(2)}) collective-permute-start(bf16[128,2048]{1,0:T(8,128)(2,1)} %get-tuple-element.21), channel_id=1, source_target_pairs={{0,1},{1,0},{2,3},{3,2},{4,5},{5,4},{6,7},{7,6},{8,9},{9,8},{10,11... | collective-permute-start | bytes 1572872 | tf_op jit(solution)/shard_map/ppermute | solution.py:201
  72.7 11.1 %collective-permute-done.8.cross = bf16[2,256,512]{2,1,0:T(8,128)(2,1)S(1)} collective-permute-done((bf16[2,256,512]{2,1,0:T(8,128)(2,1)}, bf16[2,256,512]{2,1,0:T(8,128)(2,1)S(1)}, u32[]{:S(2)}, u32[]{:S(2)}) %collective-permute-start.8) | collective-permute-done | bytes 524320 | tf_op jit(solution)/shard_map/ppermute | solution.py:251
  83.8 1.2 copy-done
  85.0 0.7 copy-done.1
  85.7 1.2 shard_map.78
  86.9 5.3 %all-to-all-start = ((f32[8,1,128]{2,1,0:T(1,128)}), f32[8,1,128]{2,1,0:T(1,128)S(1)}, u32[]{:S(2)}, u32[]{:S(2)}) async-start(f32[8,1,128]{2,1,0:T(1,128)} %bitcast.9), calls=%async_computation | async-start | bytes 8192 | tf_op jit(solution)/shard_map/all_to_all | solution.py:169
  92.3 2.0 %collective-permute-start.9 = (bf16[2,128,512]{2,1,0:T(8,128)(2,1)S(1)}, bf16[2,128,512]{2,1,0:T(8,128)(2,1)S(1)}, u32[]{:S(2)}, u32[]{:S(2)}) collective-permute-start(bf16[2,128,512]{2,1,0:T(8,128)(2,1)S(1)} %get-tuple-element.28), channel_id=1, source_target_pairs={{0,1},{1,0},{2,3},{3,2},{4,5},{5,4},{6,7},{7,6},{8,9},{9,8},{10,11... | collective-permute-start | bytes 786440 | tf_op jit(solution)/shard_map/ppermute | solution.py:201
  94.3 0.1 broadcast_select_fusion.1
  94.4 2.4 %all-to-all-done = f32[8,1,128]{2,1,0:T(1,128)S(1)} async-done(((f32[8,1,128]{2,1,0:T(1,128)}), f32[8,1,128]{2,1,0:T(1,128)S(1)}, u32[]{:S(2)}, u32[]{:S(2)}) %all-to-all-start) | async-done | bytes 4128 | tf_op jit(solution)/shard_map/all_to_all | solution.py:169
  96.8 0.6 broadcast_in_dim.13
  97.5 29.8 %all-to-all-start.1 = ((f32[64,1,128]{2,1,0:T(1,128)}), f32[64,1,128]{2,1,0:T(1,128)S(1)}, u32[]{:S(2)}, u32[]{:S(2)}) async-start(f32[64,1,128]{2,1,0:T(1,128)} %broadcast_in_dim.13), calls=%async_computation.1 | async-start | bytes 65536 | tf_op jit(solution)/shard_map/all_to_all | solution.py:169
  127.2 1.0 maximum_bitcast_fusion
  128.3 12.2 %all-to-all-done.1 = f32[64,1,128]{2,1,0:T(1,128)S(1)} async-done(((f32[64,1,128]{2,1,0:T(1,128)}), f32[64,1,128]{2,1,0:T(1,128)S(1)}, u32[]{:S(2)}, u32[]{:S(2)}) %all-to-all-start.1) | async-done | bytes 32800 | tf_op jit(solution)/shard_map/all_to_all | solution.py:169
  140.7 0.8 pad_maximum_fusion.2
  (21 shorter events, 0.2 us)
Async XLA Ops:
  1.8 10.2 %collective-permute-start = (bf16[2,128,512]{2,1,0:T(8,128)(2,1)S(1)}, bf16[2,128,512]{2,1,0:T(8,128)(2,1)S(1)}, u32[]{:S(2)}, u32[]{:S(2)}) collective-permute-start(bf16[2,128,512]{2,1,0:T(8,128)(2,1)S(1)} %pad_maximum_fusion.3), channel_id=1, source_target_pairs={{0,1},{1,0},{2,3},{3,2},{4,5},{5,4},{6,7},{7,6},{8,9},{9,8},{10,11... | collective-permute-start | bytes 786440 | tf_op jit(solution)/shard_map/ppermute | solution.py:201
  12.1 8.1 %copy-start.3 = (bf16[2,256,512]{2,1,0:T(8,128)(2,1)}, bf16[2,256,512]{2,1,0:T(8,128)(2,1)S(1)}, u32[]{:S(2)}) copy-start(bf16[2,256,512]{2,1,0:T(8,128)(2,1)S(1)} %pad_maximum_fusion.1.own) | copy-start | bytes 1572868
  12.1 8.1 %collective-permute-start.1 = (bf16[128,4096]{1,0:T(8,128)(2,1)S(1)}, bf16[128,4096]{1,0:T(8,128)(2,1)S(1)}, u32[]{:S(2)}, u32[]{:S(2)}) collective-permute-start(bf16[128,4096]{1,0:T(8,128)(2,1)S(1)} %pad_maximum_fusion), channel_id=1, source_target_pairs={{0,1},{1,0},{2,3},{3,2},{4,5},{5,4},{6,7},{7,6},{8,9},{9,8},{10,11... | collective-permute-start | bytes 3145736 | tf_op jit(solution)/shard_map/ppermute | solution.py:201
  14.1 12.6 %collective-permute-start.4 = (bf16[2,256,512]{2,1,0:T(8,128)(2,1)S(1)}, bf16[2,256,512]{2,1,0:T(8,128)(2,1)S(1)}, u32[]{:S(2)}, u32[]{:S(2)}) collective-permute-start(bf16[2,256,512]{2,1,0:T(8,128)(2,1)S(1)} %pad_maximum_fusion.1.own), channel_id=1, source_target_pairs={{0,2},{1,3},{4,6},{5,7},{8,10},{9,11},{12,14},{13,15},{16,18},{17,... | collective-permute-start | bytes 1572872 | tf_op jit(solution)/shard_map/ppermute | solution.py:210
  15.4 12.5 %collective-permute-start.3 = (bf16[2,256,512]{2,1,0:T(8,128)(2,1)S(1)}, bf16[2,256,512]{2,1,0:T(8,128)(2,1)}, u32[]{:S(2)}, u32[]{:S(2)}) collective-permute-start(bf16[2,256,512]{2,1,0:T(8,128)(2,1)S(1)} %pad_maximum_fusion.1.own), channel_id=1, source_target_pairs={{0,8},{8,16},{16,24},{24,32},{32,40},{40,48},{48,56},{56,64},{64,7... | collective-permute-start | bytes 1572872 | tf_op jit(solution)/shard_map/ppermute | solution.py:211
  17.5 21.6 %collective-permute-start.2 = (bf16[2,256,512]{2,1,0:T(8,128)(2,1)S(1)}, bf16[2,256,512]{2,1,0:T(8,128)(2,1)}, u32[]{:S(2)}, u32[]{:S(2)}) collective-permute-start(bf16[2,256,512]{2,1,0:T(8,128)(2,1)S(1)} %pad_maximum_fusion.1.own), channel_id=1, source_target_pairs={{0,10},{8,18},{16,26},{24,34},{32,42},{40,50},{48,58},{56,66},{64,... | collective-permute-start | bytes 1572872 | tf_op jit(solution)/shard_map/ppermute | solution.py:212
  20.2 1.0 copy-start.2
  26.8 12.4 %copy-start.4 = (bf16[2,256,512]{2,1,0:T(8,128)(2,1)}, bf16[2,256,512]{2,1,0:T(8,128)(2,1)S(1)}, u32[]{:S(2)}) copy-start(bf16[2,256,512]{2,1,0:T(8,128)(2,1)S(1)} %collective-permute-done.4.side) | copy-start | bytes 1572868
  55.1 17.6 %collective-permute-start.6 = (bf16[2,256,512]{2,1,0:T(8,128)(2,1)}, bf16[2,256,512]{2,1,0:T(8,128)(2,1)S(1)}, u32[]{:S(2)}, u32[]{:S(2)}) collective-permute-start(bf16[2,256,512]{2,1,0:T(8,128)(2,1)} %get-tuple-element.23), channel_id=1, source_target_pairs={{2,0},{3,1},{6,4},{7,5},{10,8},{11,9},{14,12},{15,13},{18,16},{19,... | collective-permute-start | bytes 1572872 | tf_op jit(solution)/shard_map/ppermute | solution.py:249
  56.4 16.3 %collective-permute-start.7 = (bf16[2,256,512]{2,1,0:T(8,128)(2,1)}, bf16[2,256,512]{2,1,0:T(8,128)(2,1)S(1)}, u32[]{:S(2)}, u32[]{:S(2)}) collective-permute-start(bf16[2,256,512]{2,1,0:T(8,128)(2,1)} %get-tuple-element.24), channel_id=1, source_target_pairs={{8,0},{16,8},{24,16},{32,24},{40,32},{48,40},{56,48},{64,56},{72,6... | collective-permute-start | bytes 1572872 | tf_op jit(solution)/shard_map/ppermute | solution.py:250
  57.7 26.1 %collective-permute-start.8 = (bf16[2,256,512]{2,1,0:T(8,128)(2,1)}, bf16[2,256,512]{2,1,0:T(8,128)(2,1)S(1)}, u32[]{:S(2)}, u32[]{:S(2)}) collective-permute-start(bf16[2,256,512]{2,1,0:T(8,128)(2,1)} %get-tuple-element.25), channel_id=1, source_target_pairs={{10,0},{18,8},{26,16},{34,24},{42,32},{50,40},{58,48},{66,56},{74,... | collective-permute-start | bytes 1572872 | tf_op jit(solution)/shard_map/ppermute | solution.py:251
  69.9 24.5 %collective-permute-start.5 = (bf16[128,2048]{1,0:T(8,128)(2,1)}, bf16[128,2048]{1,0:T(8,128)(2,1)S(1)}, u32[]{:S(2)}, u32[]{:S(2)}) collective-permute-start(bf16[128,2048]{1,0:T(8,128)(2,1)} %get-tuple-element.21), channel_id=1, source_target_pairs={{0,1},{1,0},{2,3},{3,2},{4,5},{5,4},{6,7},{7,6},{8,9},{9,8},{10,11... | collective-permute-start | bytes 1572872 | tf_op jit(solution)/shard_map/ppermute | solution.py:201
  83.8 1.2 copy-start
  85.0 0.7 copy-start.1
  85.7 8.6 %copy-start.5 = (bf16[128,2048]{1,0:T(8,128)(2,1)S(1)}, bf16[128,2048]{1,0:T(8,128)(2,1)}, u32[]{:S(2)}) copy-start(bf16[128,2048]{1,0:T(8,128)(2,1)} %get-tuple-element.20) | copy-start | bytes 1572868
  86.9 9.9 %all-to-all-start = ((f32[8,1,128]{2,1,0:T(1,128)}), f32[8,1,128]{2,1,0:T(1,128)S(1)}, u32[]{:S(2)}, u32[]{:S(2)}) async-start(f32[8,1,128]{2,1,0:T(1,128)} %bitcast.9), calls=%async_computation | async-start | bytes 8192 | tf_op jit(solution)/shard_map/all_to_all | solution.py:169
  92.3 48.4 %collective-permute-start.9 = (bf16[2,128,512]{2,1,0:T(8,128)(2,1)S(1)}, bf16[2,128,512]{2,1,0:T(8,128)(2,1)S(1)}, u32[]{:S(2)}, u32[]{:S(2)}) collective-permute-start(bf16[2,128,512]{2,1,0:T(8,128)(2,1)S(1)} %get-tuple-element.28), channel_id=1, source_target_pairs={{0,1},{1,0},{2,3},{3,2},{4,5},{5,4},{6,7},{7,6},{8,9},{9,8},{10,11... | collective-permute-start | bytes 786440 | tf_op jit(solution)/shard_map/ppermute | solution.py:201
  97.5 43.1 %all-to-all-start.1 = ((f32[64,1,128]{2,1,0:T(1,128)}), f32[64,1,128]{2,1,0:T(1,128)S(1)}, u32[]{:S(2)}, u32[]{:S(2)}) async-start(f32[64,1,128]{2,1,0:T(1,128)} %broadcast_in_dim.13), calls=%async_computation.1 | async-start | bytes 65536 | tf_op jit(solution)/shard_map/all_to_all | solution.py:169

commit v2 on v1

--- a/solution.py
+++ b/solution.py
@@ -52,7 +52,7 @@
 
 
 def remote_kernel(
-    place, q_mine, q_theirs, g_mine, g_theirs, own_stats, cross, same, side,
+    place, q_mine, q_theirs, g_mine, g_theirs, own_stats, side, same, cross,
     side_grad, same_grad, cross_grad, dscores, stats,
 ):
     side_bias = jnp.where(place[1] == 1, 0.0, NEG_FILL)
@@ -135,9 +135,8 @@
     squares[...] += square
 
 
-def total_kernel(own, side, same, cross, dq_squares, mine, theirs, sums):
-    total = own[...] + side[...].astype(jnp.float32)
-    total = total + same[...].astype(jnp.float32) + cross[...].astype(jnp.float32)
+def total_kernel(near, same, cross, dq_squares, mine, theirs, sums):
+    total = near[...] + same[...].astype(jnp.float32) + cross[...].astype(jnp.float32)
     total = total.astype(mine.dtype)
     half = mine.shape[1]
     mine[...] = total[:, :half]
@@ -244,7 +243,7 @@
         + [(ds_spec, jax.ShapeDtypeStruct((groups, GROUP, 3 * span, span), q.dtype)), stat],
         12 * unit,
         3 * exps,
-        *rows_in, own_stats, cross, same, side,
+        *rows_in, own_stats, side, same, cross,
     )
     from_side = lax.ppermute(side_grad, "head", side_back)
     next_same = lax.ppermute(same_grad, both, chain_back)
@@ -260,13 +259,14 @@
         *rows_in, stats, own, side, same, cross, dscores,
     )
     dq_back = swap_core(dq_theirs)
-    near = lax.axis_size("head")
+    near = own_grad + from_side.astype(jnp.float32)
+    dq_squares = jnp.sum(dq_squares, axis=0, keepdims=True)
     half_shape = jax.ShapeDtypeStruct((2, rows, own.shape[2]), q.dtype)
     total_mine, total_theirs, sums = pl.pallas_call(
         total_kernel,
-        out_shape=[half_shape, half_shape, jax.ShapeDtypeStruct((near, HEAD_SIZE), jnp.float32)],
+        out_shape=[half_shape, half_shape, jax.ShapeDtypeStruct((heads, HEAD_SIZE), jnp.float32)],
         compiler_params=pltpu.CompilerParams(vmem_limit_bytes=24 * 1024 * 1024),
-    )(own_grad, from_side, next_same, next_cross, dq_squares)
+    )(near, next_same, next_cross, dq_squares)
 
     def join(mine, theirs):
         low = jnp.where(core == 0, mine, theirs)

time: 143 us -> 134 us (0.937)
  starting transfers between devices: 60.1 us -> 53.5 us
  waiting for transfers between devices: 38.1 us -> 34.9 us
  other arithmetic: 2.79 us -> 4.97 us
  local copies, waits for them, and re-layouts: 5.97 us -> 4.05 us
    ppermute x1, waiting for transfers between devices: 11.2 us -> 0.01 us  [body(): cross = lax.ppermute(own, both, slant)]
    ppermute x1, waiting for transfers between devices: 1.17 us -> 10.2 us  [body(): same = lax.ppermute(own, both, chain)]
    all_to_all x2, starting transfers between devices: 35.1 us -> 27.6 us  [all_sum(): given = lax.all_to_all(x, axes, 0, 0, tiled=True)]
    unnamed x12 -> x8, local copies, waits for them, and re-layouts: 2.89 us -> 0.98 us
    ppermute x1, starting transfers between devices: 1.32 us -> 2.87 us  [body(): side = lax.ppermute(own, 'head', side_pairs)]
    add x0 -> x1, other arithmetic: none -> 1.47 us  [body(): near = own_grad + from_side.astype(jnp.float32)]
  transfers between devices with their start and end apart: 12 -> 12, of which waited for: 5 -> 4; matrix products, arithmetic and copies ran while one was open for 3% -> 4% of each run, Pallas kernels for 12% -> 13%
where the time goes in v2:
time: 134 us; the launch traced here: 133 us
  starting transfers between devices  53.5 us (40%)
  waiting for transfers between devices  34.9 us (26%)
  Pallas kernels  33.4 us (25%)
  other arithmetic  4.97 us (4%)
  local copies, waits for them, and re-layouts  4.05 us (3%)
  between operations  2.09 us (2%)
    pallas_call x3, Pallas kernels, call(): pl.pallas_call(kernel, grid_spec=pltpu.PrefetchScalarGridSpec(num_scalar_...  32.3 us
    all_to_all x2, starting transfers between devices, all_sum(): given = lax.all_to_all(x, axes, 0, 0, tiled=True)  27.6 us
    ppermute x4, starting transfers between devices, swap_core(): return lax.ppermute(x, 'head', core_pairs)  15.6 us
    all_to_all x2, waiting for transfers between devices, all_sum(): given = lax.all_to_all(x, axes, 0, 0, tiled=True)  14.6 us
    ppermute x1, waiting for transfers between devices, body(): same = lax.ppermute(own, both, chain)  10.2 us
    ppermute x1, waiting for transfers between devices, body(): next_cross = lax.ppermute(cross_grad, both, slant_back)  10 us
    ppermute x1, starting transfers between devices, body(): side = lax.ppermute(own, 'head', side_pairs)  2.87 us
  transfers between devices with their start and end apart: 12, of which 4 were waited for; matrix products, arithmetic and copies ran while one was open for 4% of the time, Pallas kernels for 13%

profile of v2, /device:TPU:1, one launch (start us, length us, event | category | flops | bytes accessed | tf_op | source)
XLA Modules:
  0.0 133.0 jit_solution(11924897829907142277)
XLA Ops:
  0.7 1.1 constant_dynamic-slice_fusion.2
  1.8 8.8 %collective-permute-start = (bf16[2,128,512]{2,1,0:T(8,128)(2,1)S(1)}, bf16[2,128,512]{2,1,0:T(8,128)(2,1)S(1)}, u32[]{:S(2)}, u32[]{:S(2)}) collective-permute-start(bf16[2,128,512]{2,1,0:T(8,128)(2,1)S(1)} %pad_maximum_fusion.3), channel_id=1, source_target_pairs={{0,1},{1,0},{2,3},{3,2},{4,5},{5,4},{6,7},{7,6},{8,9},{9,8},{10,11... | collective-permute-start | bytes 786440 | tf_op jit(solution)/shard_map/ppermute | solution.py:200
  10.6 1.3 dynamic-slice_bitcast_fusion
  11.9 0.1 pad_maximum_fusion
  12.0 0.0 collective-permute-done
  12.1 2.0 %collective-permute-start.1 = (bf16[128,4096]{1,0:T(8,128)(2,1)S(1)}, bf16[128,4096]{1,0:T(8,128)(2,1)S(1)}, u32[]{:S(2)}, u32[]{:S(2)}) collective-permute-start(bf16[128,4096]{1,0:T(8,128)(2,1)S(1)} %pad_maximum_fusion), channel_id=1, source_target_pairs={{0,1},{1,0},{2,3},{3,2},{4,5},{5,4},{6,7},{7,6},{8,9},{9,8},{10,11... | collective-permute-start | bytes 3145736 | tf_op jit(solution)/shard_map/ppermute | solution.py:200
  14.1 1.3 collective-permute-start.4
  15.4 2.2 %collective-permute-start.3 = (bf16[2,256,512]{2,1,0:T(8,128)(2,1)S(1)}, bf16[2,256,512]{2,1,0:T(8,128)(2,1)}, u32[]{:S(2)}, u32[]{:S(2)}) collective-permute-start(bf16[2,256,512]{2,1,0:T(8,128)(2,1)S(1)} %pad_maximum_fusion.1.own), channel_id=1, source_target_pairs={{0,8},{8,16},{16,24},{24,32},{32,40},{40,48},{48,56},{56,64},{64,7... | collective-permute-start | bytes 1572872 | tf_op jit(solution)/shard_map/ppermute | solution.py:210
  17.6 2.9 %collective-permute-start.2 = (bf16[2,256,512]{2,1,0:T(8,128)(2,1)S(1)}, bf16[2,256,512]{2,1,0:T(8,128)(2,1)}, u32[]{:S(2)}, u32[]{:S(2)}) collective-permute-start(bf16[2,256,512]{2,1,0:T(8,128)(2,1)S(1)} %pad_maximum_fusion.1.own), channel_id=1, source_target_pairs={{0,2},{1,3},{4,6},{5,7},{8,10},{9,11},{12,14},{13,15},{16,18},{17,... | collective-permute-start | bytes 1572872 | tf_op jit(solution)/shard_map/ppermute | solution.py:209
  20.5 0.6 pad_add_fusion.place
  21.1 1.0 copy-done
  22.1 5.6 %shard_map.75.own_stats = f32[4,16,256]{2,1,0:T(8,128)} custom-call(s32[3]{0:T(128)} %pad_add_fusion.place, bf16[128,4096]{1,0:T(8,128)(2,1)} %bitcast.20, bf16[128,4096]{1,0:T(8,128)(2,1)} %copy-done, bf16[128,4096]{1,0:T(8,128)(2,1)} %bitcast.23, bf16[128,4096]{1,0:T(8,128)(2,1)} %copy-done, bf16[2,256,512]{2,1,0:T(8,128)(2,1)} %copy-done.1), custom_call_target="tpu_custom_call" | custom-call | flops 536870912 | bytes 4194304 | tf_op jit(solution)/shard_map/pallas_call | solution.py:151
  27.6 10.2 %collective-permute-done.3.same = bf16[2,256,512]{2,1,0:T(8,128)(2,1)} collective-permute-done((bf16[2,256,512]{2,1,0:T(8,128)(2,1)S(1)}, bf16[2,256,512]{2,1,0:T(8,128)(2,1)}, u32[]{:S(2)}, u32[]{:S(2)}) %collective-permute-start.3) | collective-permute-done | bytes 524320 | tf_op jit(solution)/shard_map/ppermute | solution.py:210
  37.9 16.0 %shard_map.76 = (bf16[2,256,512]{2,1,0:T(8,128)(2,1)}, bf16[2,256,512]{2,1,0:T(8,128)(2,1)}, bf16[2,256,512]{2,1,0:T(8,128)(2,1)}, bf16[4,4,768,256]{3,2,1,0:T(8,128)(2,1)}, f32[4,16,256]{2,1,0:T(8,128)}) custom-call(s32[3]{0:T(128)} %pad_add_fusion.place, bf16[128,4096]{1,0:T(8,128)(2,1)} %bitcast.21, bf16[128,4096]{1,0:T(8,128)(2,1)} %copy-done, ...), custom_call_target="tpu_custom_call" | custom-call | flops 3221225472 | bytes 4194304 | tf_op jit(solution)/shard_map/pallas_call | solution.py:151
  53.9 1.3 collective-permute-start.6
  55.2 1.3 collective-permute-start.7
  56.5 1.3 collective-permute-start.8
  57.8 10.8 %shard_map.77 = (bf16[128,2048]{1,0:T(8,128)(2,1)}, bf16[128,2048]{1,0:T(8,128)(2,1)}, f32[2,256,512]{2,1,0:T(8,128)}, f32[8,128]{1,0:T(8,128)}) custom-call(s32[3]{0:T(128)} %pad_add_fusion.place, bf16[128,4096]{1,0:T(8,128)(2,1)} %bitcast.22, bf16[128,4096]{1,0:T(8,128)(2,1)} %copy-done, bf16[128,4096]{1,0:T(8,128)(2,1)} %bitcast.25, ...), custom_call_target="tpu_custom_call" | custom-call | flops 2147483648 | bytes 4194304 | tf_op jit(solution)/shard_map/pallas_call | solution.py:151
  68.6 2.8 %collective-permute-start.5 = (bf16[128,2048]{1,0:T(8,128)(2,1)}, bf16[128,2048]{1,0:T(8,128)(2,1)S(1)}, u32[]{:S(2)}, u32[]{:S(2)}) collective-permute-start(bf16[128,2048]{1,0:T(8,128)(2,1)} %get-tuple-element.21), channel_id=1, source_target_pairs={{0,1},{1,0},{2,3},{3,2},{4,5},{5,4},{6,7},{7,6},{8,9},{9,8},{10,11... | collective-permute-start | bytes 1572872 | tf_op jit(solution)/shard_map/ppermute | solution.py:200
  71.4 0.7 reduce_sum.27
  72.1 1.5 %convert_add_fusion.near = f32[2,256,512]{2,1,0:T(8,128)S(1)} fusion(f32[2,256,512]{2,1,0:T(8,128)} %get-tuple-element.22, bf16[2,256,512]{2,1,0:T(8,128)(2,1)S(1)} %collective-permute-done.6), kind=kLoop, calls=%fused_computation.2 | loop fusion | flops 524288 | bytes 2621440 | tf_op jit(solution)/shard_map/add | solution.py:262
  73.6 10.0 %collective-permute-done.8.cross = bf16[2,256,512]{2,1,0:T(8,128)(2,1)S(1)} collective-permute-done((bf16[2,256,512]{2,1,0:T(8,128)(2,1)}, bf16[2,256,512]{2,1,0:T(8,128)(2,1)S(1)}, u32[]{:S(2)}, u32[]{:S(2)}) %collective-permute-start.8) | collective-permute-done | bytes 524320 | tf_op jit(solution)/shard_map/ppermute | solution.py:250
  83.7 1.1 shard_map.78
  84.8 5.1 %all-to-all-start = ((f32[8,1,128]{2,1,0:T(1,128)}), f32[8,1,128]{2,1,0:T(1,128)S(1)}, u32[]{:S(2)}, u32[]{:S(2)}) async-start(f32[8,1,128]{2,1,0:T(1,128)} %bitcast.10), calls=%async_computation | async-start | bytes 8192 | tf_op jit(solution)/shard_map/all_to_all | solution.py:168
  89.8 2.0 %collective-permute-start.9 = (bf16[2,128,512]{2,1,0:T(8,128)(2,1)S(1)}, bf16[2,128,512]{2,1,0:T(8,128)(2,1)S(1)}, u32[]{:S(2)}, u32[]{:S(2)}) collective-permute-start(bf16[2,128,512]{2,1,0:T(8,128)(2,1)S(1)} %get-tuple-element.28), channel_id=1, source_target_pairs={{0,1},{1,0},{2,3},{3,2},{4,5},{5,4},{6,7},{7,6},{8,9},{9,8},{10,11... | collective-permute-start | bytes 786440 | tf_op jit(solution)/shard_map/ppermute | solution.py:200
  91.9 0.1 broadcast_select_fusion.1
  92.0 2.4 %all-to-all-done = f32[8,1,128]{2,1,0:T(1,128)S(1)} async-done(((f32[8,1,128]{2,1,0:T(1,128)}), f32[8,1,128]{2,1,0:T(1,128)S(1)}, u32[]{:S(2)}, u32[]{:S(2)}) %all-to-all-start) | async-done | bytes 4128 | tf_op jit(solution)/shard_map/all_to_all | solution.py:168
  94.4 0.6 broadcast_in_dim.17
  95.0 22.5 %all-to-all-start.1 = ((f32[64,1,128]{2,1,0:T(1,128)}), f32[64,1,128]{2,1,0:T(1,128)S(1)}, u32[]{:S(2)}, u32[]{:S(2)}) async-start(f32[64,1,128]{2,1,0:T(1,128)} %broadcast_in_dim.17), calls=%async_computation.1 | async-start | bytes 65536 | tf_op jit(solution)/shard_map/all_to_all | solution.py:168
  117.5 1.0 maximum_bitcast_fusion
  118.6 12.2 %all-to-all-done.1 = f32[64,1,128]{2,1,0:T(1,128)S(1)} async-done(((f32[64,1,128]{2,1,0:T(1,128)}), f32[64,1,128]{2,1,0:T(1,128)S(1)}, u32[]{:S(2)}, u32[]{:S(2)}) %all-to-all-start.1) | async-done | bytes 32800 | tf_op jit(solution)/shard_map/all_to_all | solution.py:168
  131.0 0.8 pad_maximum_fusion.2
  (19 shorter events, 0.2 us)
Async XLA Ops:
  1.8 10.2 %collective-permute-start = (bf16[2,128,512]{2,1,0:T(8,128)(2,1)S(1)}, bf16[2,128,512]{2,1,0:T(8,128)(2,1)S(1)}, u32[]{:S(2)}, u32[]{:S(2)}) collective-permute-start(bf16[2,128,512]{2,1,0:T(8,128)(2,1)S(1)} %pad_maximum_fusion.3), channel_id=1, source_target_pairs={{0,1},{1,0},{2,3},{3,2},{4,5},{5,4},{6,7},{7,6},{8,9},{9,8},{10,11... | collective-permute-start | bytes 786440 | tf_op jit(solution)/shard_map/ppermute | solution.py:200
  12.1 9.0 %copy-start.1 = (bf16[2,256,512]{2,1,0:T(8,128)(2,1)}, bf16[2,256,512]{2,1,0:T(8,128)(2,1)S(1)}, u32[]{:S(2)}) copy-start(bf16[2,256,512]{2,1,0:T(8,128)(2,1)S(1)} %pad_maximum_fusion.1.own) | copy-start | bytes 1572868
  12.1 9.0 %collective-permute-start.1 = (bf16[128,4096]{1,0:T(8,128)(2,1)S(1)}, bf16[128,4096]{1,0:T(8,128)(2,1)S(1)}, u32[]{:S(2)}, u32[]{:S(2)}) collective-permute-start(bf16[128,4096]{1,0:T(8,128)(2,1)S(1)} %pad_maximum_fusion), channel_id=1, source_target_pairs={{0,1},{1,0},{2,3},{3,2},{4,5},{5,4},{6,7},{7,6},{8,9},{9,8},{10,11... | collective-permute-start | bytes 3145736 | tf_op jit(solution)/shard_map/ppermute | solution.py:200
  14.1 13.5 %collective-permute-start.4 = (bf16[2,256,512]{2,1,0:T(8,128)(2,1)S(1)}, bf16[2,256,512]{2,1,0:T(8,128)(2,1)S(1)}, u32[]{:S(2)}, u32[]{:S(2)}) collective-permute-start(bf16[2,256,512]{2,1,0:T(8,128)(2,1)S(1)} %pad_maximum_fusion.1.own), channel_id=1, source_target_pairs={{0,10},{8,18},{16,26},{24,34},{32,42},{40,50},{48,58},{56,66},{64,... | collective-permute-start | bytes 1572872 | tf_op jit(solution)/shard_map/ppermute | solution.py:211
  15.4 22.4 %collective-permute-start.3 = (bf16[2,256,512]{2,1,0:T(8,128)(2,1)S(1)}, bf16[2,256,512]{2,1,0:T(8,128)(2,1)}, u32[]{:S(2)}, u32[]{:S(2)}) collective-permute-start(bf16[2,256,512]{2,1,0:T(8,128)(2,1)S(1)} %pad_maximum_fusion.1.own), channel_id=1, source_target_pairs={{0,8},{8,16},{16,24},{24,32},{32,40},{40,48},{48,56},{56,64},{64,7... | collective-permute-start | bytes 1572872 | tf_op jit(solution)/shard_map/ppermute | solution.py:210
  17.6 20.2 %collective-permute-start.2 = (bf16[2,256,512]{2,1,0:T(8,128)(2,1)S(1)}, bf16[2,256,512]{2,1,0:T(8,128)(2,1)}, u32[]{:S(2)}, u32[]{:S(2)}) collective-permute-start(bf16[2,256,512]{2,1,0:T(8,128)(2,1)S(1)} %pad_maximum_fusion.1.own), channel_id=1, source_target_pairs={{0,2},{1,3},{4,6},{5,7},{8,10},{9,11},{12,14},{13,15},{16,18},{17,... | collective-permute-start | bytes 1572872 | tf_op jit(solution)/shard_map/ppermute | solution.py:209
  21.1 1.0 copy-start
  27.6 10.2 %copy-start.2 = (bf16[2,256,512]{2,1,0:T(8,128)(2,1)}, bf16[2,256,512]{2,1,0:T(8,128)(2,1)S(1)}, u32[]{:S(2)}) copy-start(bf16[2,256,512]{2,1,0:T(8,128)(2,1)S(1)} %collective-permute-done.4.cross) | copy-start | bytes 1572868
  53.9 18.3 %collective-permute-start.6 = (bf16[2,256,512]{2,1,0:T(8,128)(2,1)}, bf16[2,256,512]{2,1,0:T(8,128)(2,1)S(1)}, u32[]{:S(2)}, u32[]{:S(2)}) collective-permute-start(bf16[2,256,512]{2,1,0:T(8,128)(2,1)} %get-tuple-element.23), channel_id=1, source_target_pairs={{2,0},{3,1},{6,4},{7,5},{10,8},{11,9},{14,12},{15,13},{18,16},{19,... | collective-permute-start | bytes 1572872 | tf_op jit(solution)/shard_map/ppermute | solution.py:248
  55.2 18.5 %collective-permute-start.7 = (bf16[2,256,512]{2,1,0:T(8,128)(2,1)}, bf16[2,256,512]{2,1,0:T(8,128)(2,1)S(1)}, u32[]{:S(2)}, u32[]{:S(2)}) collective-permute-start(bf16[2,256,512]{2,1,0:T(8,128)(2,1)} %get-tuple-element.24), channel_id=1, source_target_pairs={{8,0},{16,8},{24,16},{32,24},{40,32},{48,40},{56,48},{64,56},{72,6... | collective-permute-start | bytes 1572872 | tf_op jit(solution)/shard_map/ppermute | solution.py:249
  56.5 27.2 %collective-permute-start.8 = (bf16[2,256,512]{2,1,0:T(8,128)(2,1)}, bf16[2,256,512]{2,1,0:T(8,128)(2,1)S(1)}, u32[]{:S(2)}, u32[]{:S(2)}) collective-permute-start(bf16[2,256,512]{2,1,0:T(8,128)(2,1)} %get-tuple-element.25), channel_id=1, source_target_pairs={{10,0},{18,8},{26,16},{34,24},{42,32},{50,40},{58,48},{66,56},{74,... | collective-permute-start | bytes 1572872 | tf_op jit(solution)/shard_map/ppermute | solution.py:250
  68.6 23.3 %collective-permute-start.5 = (bf16[128,2048]{1,0:T(8,128)(2,1)}, bf16[128,2048]{1,0:T(8,128)(2,1)S(1)}, u32[]{:S(2)}, u32[]{:S(2)}) collective-permute-start(bf16[128,2048]{1,0:T(8,128)(2,1)} %get-tuple-element.21), channel_id=1, source_target_pairs={{0,1},{1,0},{2,3},{3,2},{4,5},{5,4},{6,7},{7,6},{8,9},{9,8},{10,11... | collective-permute-start | bytes 1572872 | tf_op jit(solution)/shard_map/ppermute | solution.py:200
  72.1 19.7 %copy-start.3 = (bf16[128,2048]{1,0:T(8,128)(2,1)S(1)}, bf16[128,2048]{1,0:T(8,128)(2,1)}, u32[]{:S(2)}) copy-start(bf16[128,2048]{1,0:T(8,128)(2,1)} %get-tuple-element.20) | copy-start | bytes 1572868
  84.8 9.6 %all-to-all-start = ((f32[8,1,128]{2,1,0:T(1,128)}), f32[8,1,128]{2,1,0:T(1,128)S(1)}, u32[]{:S(2)}, u32[]{:S(2)}) async-start(f32[8,1,128]{2,1,0:T(1,128)} %bitcast.10), calls=%async_computation | async-start | bytes 8192 | tf_op jit(solution)/shard_map/all_to_all | solution.py:168
  89.8 41.1 %collective-permute-start.9 = (bf16[2,128,512]{2,1,0:T(8,128)(2,1)S(1)}, bf16[2,128,512]{2,1,0:T(8,128)(2,1)S(1)}, u32[]{:S(2)}, u32[]{:S(2)}) collective-permute-start(bf16[2,128,512]{2,1,0:T(8,128)(2,1)S(1)} %get-tuple-element.28), channel_id=1, source_target_pairs={{0,1},{1,0},{2,3},{3,2},{4,5},{5,4},{6,7},{7,6},{8,9},{9,8},{10,11... | collective-permute-start | bytes 786440 | tf_op jit(solution)/shard_map/ppermute | solution.py:200
  95.0 35.8 %all-to-all-start.1 = ((f32[64,1,128]{2,1,0:T(1,128)}), f32[64,1,128]{2,1,0:T(1,128)S(1)}, u32[]{:S(2)}, u32[]{:S(2)}) async-start(f32[64,1,128]{2,1,0:T(1,128)} %broadcast_in_dim.17), calls=%async_computation.1 | async-start | bytes 65536 | tf_op jit(solution)/shard_map/all_to_all | solution.py:168

commit v3 on v2

--- a/solution.py
+++ b/solution.py
@@ -52,13 +52,16 @@
 
 
 def remote_kernel(
-    place, q_mine, q_theirs, g_mine, g_theirs, own_stats, side, same, cross,
+    place, q_mine, q_theirs, g_mine, g_theirs, own_stats, side, same, cross, fold_same, fold_cross,
     side_grad, same_grad, cross_grad, dscores, stats,
 ):
     side_bias = jnp.where(place[1] == 1, 0.0, NEG_FILL)
     prev_bias = jnp.where(place[2] == 1, 0.0, NEG_FILL)
     biases = (side_bias, prev_bias, prev_bias)
-    parts = (side, same, cross)
+    parts = [
+        [part[i] if fold is None else part[i] + fold[i] for i in range(2)]
+        for part, fold in ((side, None), (same, fold_same), (cross, fold_cross))
+    ]
     rows = side.shape[1]
     key_sums = [None] * len(parts)
     value_sums = [None] * len(parts)
@@ -96,13 +99,14 @@
 
 
 def rest_kernel(
-    place, q_mine, q_theirs, g_mine, g_theirs, stats, own, side, same, cross, dscores,
+    place, q_mine, q_theirs, g_mine, g_theirs, stats, own, side, same, cross, fold_same, fold_cross, dscores,
     dq_mine, dq_theirs, own_grad, squares,
 ):
     half = dq_mine.shape[0]
     rows = 2 * half
     key_sum = value_sum = None
     square = jnp.zeros((8, HEAD_SIZE), jnp.float32)
+    keys = (side[0], same[0] + fold_same[0], cross[0] + fold_cross[0])
     for head in range(GROUP):
         q = pair(q_mine, q_theirs, head)
         g = pair(g_mine, g_theirs, head)
@@ -117,8 +121,8 @@
         value_sum = dv if head == 0 else value_sum + dv
         key_sum = dk if head == 0 else key_sum + dk
         dq = dot(ds, own[0], TN)
-        for i, part in enumerate((side, same, cross)):
-            dq = dq + dot(dscores[0, head, i * rows : (i + 1) * rows], part[0], TN)
+        for i, key in enumerate(keys):
+            dq = dq + dot(dscores[0, head, i * rows : (i + 1) * rows], key, TN)
         dq = (dq * SCALE).astype(dq_mine.dtype)
         cols = slice(head * HEAD_SIZE, (head + 1) * HEAD_SIZE)
         dq_mine[:, cols] = dq[:half]
@@ -135,8 +139,9 @@
     squares[...] += square
 
 
-def total_kernel(near, same, cross, dq_squares, mine, theirs, sums):
+def total_kernel(near, same, cross, fold, dq_squares, mine, theirs, sums):
     total = near[...] + same[...].astype(jnp.float32) + cross[...].astype(jnp.float32)
+    total = total + fold[...].astype(jnp.float32)
     total = total.astype(mine.dtype)
     half = mine.shape[1]
     mine[...] = total[:, :half]
@@ -189,11 +194,15 @@
     chain = []
     for h in range(quarter):
         chain += [(flat(c, h), flat(c + 1, h)) for c in range(contexts - 1)]
-        chain += [(flat(contexts - 1, h), flat(contexts - 1, h + quarter))]
         chain += [(flat(c, h + quarter), flat(c - 1, h + quarter)) for c in range(1, contexts)]
     slant = [(source, target ^ 2) for source, target in chain]
+    last = contexts - 1
+    fold_far = [(flat(last, h), flat(last, (h + quarter) ^ 2)) for h in range(quarter)]
+    fold_near = [(flat(last, h), flat(last, h ^ 2)) for h in range(quarter, heads)]
+    fold_near_back = [(flat(last, h), flat(last, h ^ 2)) for h in range(quarter)]
+    fold_far_back = [(target, source) for source, target in fold_far]
     chain_back = [(target, source) for source, target in chain]
-    slant_back = [(target, source) for source, target in slant]
+    slant_back = [(target, source) for source, target in slant] + fold_far_back
     both = ("ctx", "head")
 
     def swap_core(x):
@@ -206,6 +215,7 @@
     rows = q.shape[0]
     kv_theirs = swap_core(jnp.stack([cut(k, 1 - core), cut(v, 1 - core)]))
     own = jnp.concatenate([jnp.stack([cut(k, core), cut(v, core)]), kv_theirs], axis=1)
+    fold_cross = lax.ppermute(own, both, fold_far)
     side = lax.ppermute(own, "head", side_pairs)
     same = lax.ppermute(own, both, chain)
     cross = lax.ppermute(own, both, slant)
@@ -235,29 +245,34 @@
     (own_stats,) = call(
         own_kernel, groups, qg_specs + [kv_spec], [stat], 2 * unit, exps, *rows_in, own
     )
+    fold_first, own_stats = lax.optimization_barrier((fold_cross, own_stats))
+    fold_same = lax.ppermute(fold_first, both, fold_near)
     side_grad, same_grad, cross_grad, dscores, stats = call(
         remote_kernel,
         groups,
-        qg_specs + [stat_spec] + [kv_spec] * 3,
+        qg_specs + [stat_spec] + [kv_spec] * 5,
         [grad] * 3
         + [(ds_spec, jax.ShapeDtypeStruct((groups, GROUP, 3 * span, span), q.dtype)), stat],
         12 * unit,
         3 * exps,
-        *rows_in, own_stats, side, same, cross,
+        *rows_in, own_stats, side, same, cross, fold_same, fold_cross,
     )
+    fold_grad = lax.ppermute(same_grad, both, fold_far_back)
     from_side = lax.ppermute(side_grad, "head", side_back)
     next_same = lax.ppermute(same_grad, both, chain_back)
     next_cross = lax.ppermute(cross_grad, both, slant_back)
     dq_mine, dq_theirs, own_grad, dq_squares = call(
         rest_kernel,
         groups,
-        qg_specs + [stat_spec, kv_spec] + [k_spec] * 3 + [ds_spec],
+        qg_specs + [stat_spec, kv_spec] + [k_spec] * 5 + [ds_spec],
         [part, part, (kv_spec, jax.ShapeDtypeStruct(own.shape, jnp.float32))]
         + [(square_spec, jax.ShapeDtypeStruct((8, HEAD_SIZE), jnp.float32))],
         8 * unit,
         exps,
-        *rows_in, stats, own, side, same, cross, dscores,
+        *rows_in, stats, own, side, same, cross, fold_same, fold_cross, dscores,
     )
+    fold_grad, dq_squares = lax.optimization_barrier((fold_grad, dq_squares))
+    from_fold = lax.ppermute(fold_grad, both, fold_near_back)
     dq_back = swap_core(dq_theirs)
     near = own_grad + from_side.astype(jnp.float32)
     dq_squares = jnp.sum(dq_squares, axis=0, keepdims=True)
@@ -266,7 +281,7 @@
         total_kernel,
         out_shape=[half_shape, half_shape, jax.ShapeDtypeStruct((heads, HEAD_SIZE), jnp.float32)],
         compiler_params=pltpu.CompilerParams(vmem_limit_bytes=24 * 1024 * 1024),
-    )(near, next_same, next_cross, dq_squares)
+    )(near, next_same, next_cross, from_fold, dq_squares)
 
     def join(mine, theirs):
         low = jnp.where(core == 0, mine, theirs)

time: 134 us -> 133 us (level)
    all_to_all x2, starting transfers between devices: 27.6 us -> 22.9 us  [all_sum(): given = lax.all_to_all(x, axes, 0, 0, tiled=True)]
    ppermute x0 -> x4, starting transfers between devices: none -> 3.6 us  [the longest x1 1.52 us: body(): fold_grad = lax.ppermute(same_grad, both, fold_far_back)]
  transfers between devices with their start and end apart: 12 -> 16, of which waited for: 4 -> 4; matrix products, arithmetic and copies ran while one was open for 4% -> 5% of each run, Pallas kernels for 13% -> 13%
where the time goes in v3:
time: 133 us; the launch traced here: 132 us
  starting transfers between devices  52.4 us (39%)
  waiting for transfers between devices  34.1 us (26%)
  Pallas kernels  33.7 us (25%)
  other arithmetic  5.02 us (4%)
  local copies, waits for them, and re-layouts  4.9 us (4%)
  between operations  2.18 us (2%)
    pallas_call x3, Pallas kernels, call(): pl.pallas_call(kernel, grid_spec=pltpu.PrefetchScalarGridSpec(num_scalar_...  32.5 us
    all_to_all x2, starting transfers between devices, all_sum(): given = lax.all_to_all(x, axes, 0, 0, tiled=True)  22.9 us
    ppermute x4, starting transfers between devices, swap_core(): return lax.ppermute(x, 'head', core_pairs)  15.7 us
    all_to_all x2, waiting for transfers between devices, all_sum(): given = lax.all_to_all(x, axes, 0, 0, tiled=True)  14.6 us
    ppermute x1, waiting for transfers between devices, body(): same = lax.ppermute(own, both, chain)  10.1 us
    ppermute x1, waiting for transfers between devices, body(): next_cross = lax.ppermute(cross_grad, both, slant_back)  9.34 us
    ppermute x1, starting transfers between devices, body(): side = lax.ppermute(own, 'head', side_pairs)  2.87 us
  transfers between devices with their start and end apart: 16, of which 4 were waited for; matrix products, arithmetic and copies ran while one was open for 5% of the time, Pallas kernels for 13%

profile of v3, /device:TPU:1, one launch (start us, length us, event | category | flops | bytes accessed | tf_op | source)
XLA Modules:
  0.0 132.3 jit_solution(6597812541319456081)
XLA Ops:
  0.7 1.1 constant_dynamic-slice_fusion.2
  1.8 8.8 %collective-permute-start = (bf16[2,128,512]{2,1,0:T(8,128)(2,1)S(1)}, bf16[2,128,512]{2,1,0:T(8,128)(2,1)S(1)}, u32[]{:S(2)}, u32[]{:S(2)}) collective-permute-start(bf16[2,128,512]{2,1,0:T(8,128)(2,1)S(1)} %pad_maximum_fusion.3), channel_id=1, source_target_pairs={{0,1},{1,0},{2,3},{3,2},{4,5},{5,4},{6,7},{7,6},{8,9},{9,8},{10,11... | collective-permute-start | bytes 786440 | tf_op jit(solution)/shard_map/ppermute | solution.py:209
  10.6 1.3 dynamic-slice_bitcast_fusion
  12.1 2.0 %collective-permute-start.1 = (bf16[128,4096]{1,0:T(8,128)(2,1)S(1)}, bf16[128,4096]{1,0:T(8,128)(2,1)S(1)}, u32[]{:S(2)}, u32[]{:S(2)}) collective-permute-start(bf16[128,4096]{1,0:T(8,128)(2,1)S(1)} %pad_maximum_fusion), channel_id=1, source_target_pairs={{0,1},{1,0},{2,3},{3,2},{4,5},{5,4},{6,7},{7,6},{8,9},{9,8},{10,11... | collective-permute-start | bytes 3145736 | tf_op jit(solution)/shard_map/ppermute | solution.py:209
  14.1 0.7 collective-permute-start.2
  15.5 1.3 collective-permute-start.5
  16.8 2.2 %collective-permute-start.4 = (bf16[2,256,512]{2,1,0:T(8,128)(2,1)S(1)}, bf16[2,256,512]{2,1,0:T(8,128)(2,1)}, u32[]{:S(2)}, u32[]{:S(2)}) collective-permute-start(bf16[2,256,512]{2,1,0:T(8,128)(2,1)S(1)} %pad_maximum_fusion.1.own), channel_id=1, source_target_pairs={{0,8},{8,16},{16,24},{24,32},{32,40},{40,48},{48,56},{56,64},{64,7... | collective-permute-start | bytes 1572872 | tf_op jit(solution)/shard_map/ppermute | solution.py:220
  19.0 2.9 %collective-permute-start.3 = (bf16[2,256,512]{2,1,0:T(8,128)(2,1)S(1)}, bf16[2,256,512]{2,1,0:T(8,128)(2,1)}, u32[]{:S(2)}, u32[]{:S(2)}) collective-permute-start(bf16[2,256,512]{2,1,0:T(8,128)(2,1)S(1)} %pad_maximum_fusion.1.own), channel_id=1, source_target_pairs={{0,2},{1,3},{4,6},{5,7},{8,10},{9,11},{12,14},{13,15},{16,18},{17,... | collective-permute-start | bytes 1572872 | tf_op jit(solution)/shard_map/ppermute | solution.py:219
  21.9 1.0 copy-done
  22.9 5.6 %shard_map.75.own_stats = f32[4,16,256]{2,1,0:T(8,128)} custom-call(s32[3]{0:T(128)} %pad_add_fusion.place, bf16[128,4096]{1,0:T(8,128)(2,1)} %bitcast.20, bf16[128,4096]{1,0:T(8,128)(2,1)} %copy-done, bf16[128,4096]{1,0:T(8,128)(2,1)} %bitcast.23, bf16[128,4096]{1,0:T(8,128)(2,1)} %copy-done, bf16[2,256,512]{2,1,0:T(8,128)(2,1)} %copy-done.1), custom_call_target="tpu_custom_call" | custom-call | flops 536870912 | bytes 4194304 | tf_op jit(solution)/shard_map/pallas_call | solution.py:156
  28.4 0.7 collective-permute-start.6
  29.2 10.1 %collective-permute-done.4.same = bf16[2,256,512]{2,1,0:T(8,128)(2,1)} collective-permute-done((bf16[2,256,512]{2,1,0:T(8,128)(2,1)S(1)}, bf16[2,256,512]{2,1,0:T(8,128)(2,1)}, u32[]{:S(2)}, u32[]{:S(2)}) %collective-permute-start.4) | collective-permute-done | bytes 524320 | tf_op jit(solution)/shard_map/ppermute | solution.py:220
  39.3 0.8 copy-done.5
  40.1 16.0 %shard_map.76 = (bf16[2,256,512]{2,1,0:T(8,128)(2,1)}, bf16[2,256,512]{2,1,0:T(8,128)(2,1)}, bf16[2,256,512]{2,1,0:T(8,128)(2,1)}, bf16[4,4,768,256]{3,2,1,0:T(8,128)(2,1)}, f32[4,16,256]{2,1,0:T(8,128)}) custom-call(s32[3]{0:T(128)} %pad_add_fusion.place, bf16[128,4096]{1,0:T(8,128)(2,1)} %bitcast.21, bf16[128,4096]{1,0:T(8,128)(2,1)} %copy-done, ...), custom_call_target="tpu_custom_call" | custom-call | flops 3221225472 | bytes 4194304 | tf_op jit(solution)/shard_map/pallas_call | solution.py:156
  56.2 1.5 %collective-permute-start.11 = (bf16[2,256,512]{2,1,0:T(8,128)(2,1)}, bf16[2,256,512]{2,1,0:T(8,128)(2,1)}, u32[]{:S(2)}, u32[]{:S(2)}) collective-permute-start(bf16[2,256,512]{2,1,0:T(8,128)(2,1)} %get-tuple-element.30), channel_id=1, source_target_pairs={{254,248},{255,249},{252,250},{253,251},{510,504},{511,505},{508,5... | collective-permute-start | bytes 1572872 | tf_op jit(solution)/shard_map/ppermute | solution.py:260
  57.7 1.3 collective-permute-start.8
  59.0 1.3 collective-permute-start.9
  60.3 1.3 collective-permute-start.10
  61.6 10.9 %shard_map.77 = (bf16[128,2048]{1,0:T(8,128)(2,1)}, bf16[128,2048]{1,0:T(8,128)(2,1)}, f32[2,256,512]{2,1,0:T(8,128)}, f32[8,128]{1,0:T(8,128)}) custom-call(s32[3]{0:T(128)} %pad_add_fusion.place, bf16[128,4096]{1,0:T(8,128)(2,1)} %bitcast.22, bf16[128,4096]{1,0:T(8,128)(2,1)} %copy-done, bf16[128,4096]{1,0:T(8,128)(2,1)} %bitcast.25, ...), custom_call_target="tpu_custom_call" | custom-call | flops 2147483648 | bytes 4194304 | tf_op jit(solution)/shard_map/pallas_call | solution.py:156
  72.5 0.7 collective-permute-start.12
  73.2 2.8 %collective-permute-start.7 = (bf16[128,2048]{1,0:T(8,128)(2,1)}, bf16[128,2048]{1,0:T(8,128)(2,1)S(1)}, u32[]{:S(2)}, u32[]{:S(2)}) collective-permute-start(bf16[128,2048]{1,0:T(8,128)(2,1)} %get-tuple-element.27), channel_id=1, source_target_pairs={{0,1},{1,0},{2,3},{3,2},{4,5},{5,4},{6,7},{7,6},{8,9},{9,8},{10,11... | collective-permute-start | bytes 1572872 | tf_op jit(solution)/shard_map/ppermute | solution.py:209
  76.0 0.7 reduce_sum.27
  76.7 1.5 %convert_add_fusion.near = f32[2,256,512]{2,1,0:T(8,128)S(1)} fusion(f32[2,256,512]{2,1,0:T(8,128)} %get-tuple-element.28, bf16[2,256,512]{2,1,0:T(8,128)(2,1)S(1)} %collective-permute-done.8), kind=kLoop, calls=%fused_computation.2 | loop fusion | flops 524288 | bytes 2621440 | tf_op jit(solution)/shard_map/add | solution.py:277
  78.2 9.3 %collective-permute-done.10.cross = bf16[2,256,512]{2,1,0:T(8,128)(2,1)S(1)} collective-permute-done((bf16[2,256,512]{2,1,0:T(8,128)(2,1)}, bf16[2,256,512]{2,1,0:T(8,128)(2,1)S(1)}, u32[]{:S(2)}, u32[]{:S(2)}) %collective-permute-start.10) | collective-permute-done | bytes 524320 | tf_op jit(solution)/shard_map/ppermute | solution.py:263
  87.5 1.2 shard_map.78
  88.8 5.0 %all-to-all-start = ((f32[8,1,128]{2,1,0:T(1,128)}), f32[8,1,128]{2,1,0:T(1,128)S(1)}, u32[]{:S(2)}, u32[]{:S(2)}) async-start(f32[8,1,128]{2,1,0:T(1,128)} %bitcast.10), calls=%async_computation | async-start | bytes 8192 | tf_op jit(solution)/shard_map/all_to_all | solution.py:173
  93.9 2.0 %collective-permute-start.13 = (bf16[2,128,512]{2,1,0:T(8,128)(2,1)S(1)}, bf16[2,128,512]{2,1,0:T(8,128)(2,1)S(1)}, u32[]{:S(2)}, u32[]{:S(2)}) collective-permute-start(bf16[2,128,512]{2,1,0:T(8,128)(2,1)S(1)} %get-tuple-element.36), channel_id=1, source_target_pairs={{0,1},{1,0},{2,3},{3,2},{4,5},{5,4},{6,7},{7,6},{8,9},{9,8},{10,11... | collective-permute-start | bytes 786440 | tf_op jit(solution)/shard_map/ppermute | solution.py:209
  95.9 2.4 %all-to-all-done = f32[8,1,128]{2,1,0:T(1,128)S(1)} async-done(((f32[8,1,128]{2,1,0:T(1,128)}), f32[8,1,128]{2,1,0:T(1,128)S(1)}, u32[]{:S(2)}, u32[]{:S(2)}) %all-to-all-start) | async-done | bytes 4128 | tf_op jit(solution)/shard_map/all_to_all | solution.py:173
  99.0 17.8 %all-to-all-start.1 = ((f32[64,1,128]{2,1,0:T(1,128)}), f32[64,1,128]{2,1,0:T(1,128)S(1)}, u32[]{:S(2)}, u32[]{:S(2)}) async-start(f32[64,1,128]{2,1,0:T(1,128)} %broadcast_in_dim.17), calls=%async_computation.1 | async-start | bytes 65536 | tf_op jit(solution)/shard_map/all_to_all | solution.py:173
  116.8 1.0 maximum_bitcast_fusion
  117.9 12.2 %all-to-all-done.1 = f32[64,1,128]{2,1,0:T(1,128)S(1)} async-done(((f32[64,1,128]{2,1,0:T(1,128)}), f32[64,1,128]{2,1,0:T(1,128)S(1)}, u32[]{:S(2)}, u32[]{:S(2)}) %all-to-all-start.1) | async-done | bytes 32800 | tf_op jit(solution)/shard_map/all_to_all | solution.py:173
  130.3 0.8 pad_maximum_fusion.2
  (31 shorter events, 1.7 us)
Async XLA Ops:
  1.8 10.2 %collective-permute-start = (bf16[2,128,512]{2,1,0:T(8,128)(2,1)S(1)}, bf16[2,128,512]{2,1,0:T(8,128)(2,1)S(1)}, u32[]{:S(2)}, u32[]{:S(2)}) collective-permute-start(bf16[2,128,512]{2,1,0:T(8,128)(2,1)S(1)} %pad_maximum_fusion.3), channel_id=1, source_target_pairs={{0,1},{1,0},{2,3},{3,2},{4,5},{5,4},{6,7},{7,6},{8,9},{9,8},{10,11... | collective-permute-start | bytes 786440 | tf_op jit(solution)/shard_map/ppermute | solution.py:209
  12.1 9.8 %copy-start.1 = (bf16[2,256,512]{2,1,0:T(8,128)(2,1)}, bf16[2,256,512]{2,1,0:T(8,128)(2,1)S(1)}, u32[]{:S(2)}) copy-start(bf16[2,256,512]{2,1,0:T(8,128)(2,1)S(1)} %pad_maximum_fusion.1.own) | copy-start | bytes 1572868
  12.1 9.8 %collective-permute-start.1 = (bf16[128,4096]{1,0:T(8,128)(2,1)S(1)}, bf16[128,4096]{1,0:T(8,128)(2,1)S(1)}, u32[]{:S(2)}, u32[]{:S(2)}) collective-permute-start(bf16[128,4096]{1,0:T(8,128)(2,1)S(1)} %pad_maximum_fusion), channel_id=1, source_target_pairs={{0,1},{1,0},{2,3},{3,2},{4,5},{5,4},{6,7},{7,6},{8,9},{9,8},{10,11... | collective-permute-start | bytes 3145736 | tf_op jit(solution)/shard_map/ppermute | solution.py:209
  14.1 14.3 %collective-permute-start.2 = (bf16[2,256,512]{2,1,0:T(8,128)(2,1)S(1)}, bf16[2,256,512]{2,1,0:T(8,128)(2,1)S(1)}, u32[]{:S(2)}, u32[]{:S(2)}) collective-permute-start(bf16[2,256,512]{2,1,0:T(8,128)(2,1)S(1)} %pad_maximum_fusion.1.own), channel_id=1, source_target_pairs={{248,254},{249,255},{250,252},{251,253},{504,510},{505,511},{506,5... | collective-permute-start | bytes 1572872 | tf_op jit(solution)/shard_map/ppermute | solution.py:218
  15.5 13.6 %collective-permute-start.5 = (bf16[2,256,512]{2,1,0:T(8,128)(2,1)S(1)}, bf16[2,256,512]{2,1,0:T(8,128)(2,1)S(1)}, u32[]{:S(2)}, u32[]{:S(2)}) collective-permute-start(bf16[2,256,512]{2,1,0:T(8,128)(2,1)S(1)} %pad_maximum_fusion.1.own), channel_id=1, source_target_pairs={{0,10},{8,18},{16,26},{24,34},{32,42},{40,50},{48,58},{56,66},{64,... | collective-permute-start | bytes 1572872 | tf_op jit(solution)/shard_map/ppermute | solution.py:221
  16.8 22.4 %collective-permute-start.4 = (bf16[2,256,512]{2,1,0:T(8,128)(2,1)S(1)}, bf16[2,256,512]{2,1,0:T(8,128)(2,1)}, u32[]{:S(2)}, u32[]{:S(2)}) collective-permute-start(bf16[2,256,512]{2,1,0:T(8,128)(2,1)S(1)} %pad_maximum_fusion.1.own), channel_id=1, source_target_pairs={{0,8},{8,16},{16,24},{24,32},{32,40},{40,48},{48,56},{56,64},{64,7... | collective-permute-start | bytes 1572872 | tf_op jit(solution)/shard_map/ppermute | solution.py:220
  19.0 20.3 %collective-permute-start.3 = (bf16[2,256,512]{2,1,0:T(8,128)(2,1)S(1)}, bf16[2,256,512]{2,1,0:T(8,128)(2,1)}, u32[]{:S(2)}, u32[]{:S(2)}) collective-permute-start(bf16[2,256,512]{2,1,0:T(8,128)(2,1)S(1)} %pad_maximum_fusion.1.own), channel_id=1, source_target_pairs={{0,2},{1,3},{4,6},{5,7},{8,10},{9,11},{12,14},{13,15},{16,18},{17,... | collective-permute-start | bytes 1572872 | tf_op jit(solution)/shard_map/ppermute | solution.py:219
  21.9 1.0 copy-start
  28.4 10.9 %copy-start.3 = (bf16[2,256,512]{2,1,0:T(8,128)(2,1)}, bf16[2,256,512]{2,1,0:T(8,128)(2,1)S(1)}, u32[]{:S(2)}) copy-start(bf16[2,256,512]{2,1,0:T(8,128)(2,1)S(1)} %collective-permute-done.2.fold_cross) | copy-start | bytes 1572868
  28.4 10.8 %collective-permute-start.6 = (bf16[2,256,512]{2,1,0:T(8,128)(2,1)S(1)}, bf16[2,256,512]{2,1,0:T(8,128)(2,1)S(1)}, u32[]{:S(2)}, u32[]{:S(2)}) collective-permute-start(bf16[2,256,512]{2,1,0:T(8,128)(2,1)S(1)} %collective-permute-done.2.fold_cross), channel_id=1, source_target_pairs={{252,254},{253,255},{254,252},{255,253},{508,510},{509,511},{510,5... | collective-permute-start | bytes 1572872 | tf_op jit(solution)/shard_map/ppermute | solution.py:249
  29.1 10.1 %copy-start.4 = (bf16[2,256,512]{2,1,0:T(8,128)(2,1)}, bf16[2,256,512]{2,1,0:T(8,128)(2,1)S(1)}, u32[]{:S(2)}) copy-start(bf16[2,256,512]{2,1,0:T(8,128)(2,1)S(1)} %collective-permute-done.5.cross) | copy-start | bytes 1572868
  39.3 0.9 copy-start.5
  56.2 16.3 %collective-permute-start.11 = (bf16[2,256,512]{2,1,0:T(8,128)(2,1)}, bf16[2,256,512]{2,1,0:T(8,128)(2,1)}, u32[]{:S(2)}, u32[]{:S(2)}) collective-permute-start(bf16[2,256,512]{2,1,0:T(8,128)(2,1)} %get-tuple-element.30), channel_id=1, source_target_pairs={{254,248},{255,249},{252,250},{253,251},{510,504},{511,505},{508,5... | collective-permute-start | bytes 1572872 | tf_op jit(solution)/shard_map/ppermute | solution.py:260
  57.7 19.0 %collective-permute-start.8 = (bf16[2,256,512]{2,1,0:T(8,128)(2,1)}, bf16[2,256,512]{2,1,0:T(8,128)(2,1)S(1)}, u32[]{:S(2)}, u32[]{:S(2)}) collective-permute-start(bf16[2,256,512]{2,1,0:T(8,128)(2,1)} %get-tuple-element.29), channel_id=1, source_target_pairs={{2,0},{3,1},{6,4},{7,5},{10,8},{11,9},{14,12},{15,13},{18,16},{19,... | collective-permute-start | bytes 1572872 | tf_op jit(solution)/shard_map/ppermute | solution.py:261
  59.0 28.5 %collective-permute-start.9 = (bf16[2,256,512]{2,1,0:T(8,128)(2,1)}, bf16[2,256,512]{2,1,0:T(8,128)(2,1)S(1)}, u32[]{:S(2)}, u32[]{:S(2)}) collective-permute-start(bf16[2,256,512]{2,1,0:T(8,128)(2,1)} %get-tuple-element.30), channel_id=1, source_target_pairs={{8,0},{16,8},{24,16},{32,24},{40,32},{48,40},{56,48},{64,56},{72,6... | collective-permute-start | bytes 1572872 | tf_op jit(solution)/shard_map/ppermute | solution.py:262
  60.3 27.2 %collective-permute-start.10 = (bf16[2,256,512]{2,1,0:T(8,128)(2,1)}, bf16[2,256,512]{2,1,0:T(8,128)(2,1)S(1)}, u32[]{:S(2)}, u32[]{:S(2)}) collective-permute-start(bf16[2,256,512]{2,1,0:T(8,128)(2,1)} %get-tuple-element.31), channel_id=1, source_target_pairs={{10,0},{18,8},{26,16},{34,24},{42,32},{50,40},{58,48},{66,56},{74,... | collective-permute-start | bytes 1572872 | tf_op jit(solution)/shard_map/ppermute | solution.py:263
  72.5 15.1 %collective-permute-start.12 = (bf16[2,256,512]{2,1,0:T(8,128)(2,1)}, bf16[2,256,512]{2,1,0:T(8,128)(2,1)S(1)}, u32[]{:S(2)}, u32[]{:S(2)}) collective-permute-start(bf16[2,256,512]{2,1,0:T(8,128)(2,1)} %collective-permute-done.11), channel_id=1, source_target_pairs={{248,250},{249,251},{250,248},{251,249},{504,506},{505,507},{506,5... | collective-permute-start | bytes 1572872 | tf_op jit(solution)/shard_map/ppermute | solution.py:275
  73.2 20.7 %collective-permute-start.7 = (bf16[128,2048]{1,0:T(8,128)(2,1)}, bf16[128,2048]{1,0:T(8,128)(2,1)S(1)}, u32[]{:S(2)}, u32[]{:S(2)}) collective-permute-start(bf16[128,2048]{1,0:T(8,128)(2,1)} %get-tuple-element.27), channel_id=1, source_target_pairs={{0,1},{1,0},{2,3},{3,2},{4,5},{5,4},{6,7},{7,6},{8,9},{9,8},{10,11... | collective-permute-start | bytes 1572872 | tf_op jit(solution)/shard_map/ppermute | solution.py:209
  76.7 17.1 %copy-start.2 = (bf16[128,2048]{1,0:T(8,128)(2,1)S(1)}, bf16[128,2048]{1,0:T(8,128)(2,1)}, u32[]{:S(2)}) copy-start(bf16[128,2048]{1,0:T(8,128)(2,1)} %get-tuple-element.26) | copy-start | bytes 1572868
  88.8 9.6 %all-to-all-start = ((f32[8,1,128]{2,1,0:T(1,128)}), f32[8,1,128]{2,1,0:T(1,128)S(1)}, u32[]{:S(2)}, u32[]{:S(2)}) async-start(f32[8,1,128]{2,1,0:T(1,128)} %bitcast.10), calls=%async_computation | async-start | bytes 8192 | tf_op jit(solution)/shard_map/all_to_all | solution.py:173
  93.9 36.3 %collective-permute-start.13 = (bf16[2,128,512]{2,1,0:T(8,128)(2,1)S(1)}, bf16[2,128,512]{2,1,0:T(8,128)(2,1)S(1)}, u32[]{:S(2)}, u32[]{:S(2)}) collective-permute-start(bf16[2,128,512]{2,1,0:T(8,128)(2,1)S(1)} %get-tuple-element.36), channel_id=1, source_target_pairs={{0,1},{1,0},{2,3},{3,2},{4,5},{5,4},{6,7},{7,6},{8,9},{9,8},{10,11... | collective-permute-start | bytes 786440 | tf_op jit(solution)/shard_map/ppermute | solution.py:209
  99.0 31.1 %all-to-all-start.1 = ((f32[64,1,128]{2,1,0:T(1,128)}), f32[64,1,128]{2,1,0:T(1,128)S(1)}, u32[]{:S(2)}, u32[]{:S(2)}) async-start(f32[64,1,128]{2,1,0:T(1,128)} %broadcast_in_dim.17), calls=%async_computation.1 | async-start | bytes 65536 | tf_op jit(solution)/shard_map/all_to_all | solution.py:173

commit v4 on v3

--- a/solution.py
+++ b/solution.py
@@ -13,7 +13,7 @@
 NEG_FILL = -1e30
 SCALE = HEAD_SIZE**-0.5
 RATE = SCALE * math.log2(math.e)
-VMEM = 60 * 1024 * 1024
+VMEM = 63 * 1024 * 1024
 NT = (((1,), (1,)), ((), ()))
 NN = (((1,), (0,)), ((), ()))
 TN = (((0,), (0,)), ((), ()))
@@ -180,10 +180,6 @@
     quarter = heads // 2
     ctx, head = lax.axis_index("ctx"), lax.axis_index("head")
     core = head % 2
-    is_back = head >= quarter
-    place = jnp.stack(
-        [core, (head // 2) % 2, jnp.where((ctx > 0) | is_back, 1, 0)]
-    ).astype(jnp.int32)
     core_pairs = [(h, h ^ 1) for h in range(heads)]
     side_pairs = [(h, h ^ 2) for h in range(heads) if h & 2 == 0]
     side_back = [(target, source) for source, target in side_pairs]
@@ -222,6 +218,10 @@
     qg_theirs = jnp.concatenate([cut(q, 1 - core), cut(g, 1 - core)], axis=1)
     qg_theirs, own_late = lax.optimization_barrier((qg_theirs, own))
     qg_theirs = swap_core(qg_theirs)
+    late_head, qg_theirs = lax.optimization_barrier((head, qg_theirs))
+    place = jnp.stack(
+        [late_head % 2, (late_head // 2) % 2, jnp.where((ctx > 0) | (late_head >= quarter), 1, 0)]
+    ).astype(jnp.int32)
 
     groups = own.shape[2] // HEAD_SIZE
     wide = GROUP * HEAD_SIZE

time: 133 us -> 134 us (level)
  local copies, waits for them, and re-layouts: 4.9 us -> 3.08 us
  starting transfers between devices: 52.4 us -> 53.9 us
    unnamed x12 -> x2, local copies, waits for them, and re-layouts: 1.83 us -> 0.01 us
  transfers between devices with their start and end apart: 16 -> 16, of which waited for: 4 -> 4; matrix products, arithmetic and copies ran while one was open for 5% -> 5% of each run, Pallas kernels for 13% -> 14%
where the time goes in v4:
time: 134 us; the launch traced here: 133 us
  starting transfers between devices  53.9 us (40%)
  Pallas kernels  34.7 us (26%)
  waiting for transfers between devices  33.3 us (25%)
  other arithmetic  6.28 us (5%)
  local copies, waits for them, and re-layouts  3.08 us (2%)
  between operations  2.06 us (2%)
    pallas_call x3, Pallas kernels, call(): pl.pallas_call(kernel, grid_spec=pltpu.PrefetchScalarGridSpec(num_scalar_...  32.4 us
    all_to_all x2, starting transfers between devices, all_sum(): given = lax.all_to_all(x, axes, 0, 0, tiled=True)  22.9 us
    ppermute x4, starting transfers between devices, swap_core(): return lax.ppermute(x, 'head', core_pairs)  15.6 us
    all_to_all x2, waiting for transfers between devices, all_sum(): given = lax.all_to_all(x, axes, 0, 0, tiled=True)  13.5 us
    ppermute x1, waiting for transfers between devices, body(): next_cross = lax.ppermute(cross_grad, both, slant_back)  10.2 us
    ppermute x1, waiting for transfers between devices, body(): same = lax.ppermute(own, both, chain)  9.64 us
  transfers between devices with their start and end apart: 16, of which 4 were waited for; matrix products, arithmetic and copies ran while one was open for 5% of the time, Pallas kernels for 14%

profile of v4, /device:TPU:1, one launch (start us, length us, event | category | flops | bytes accessed | tf_op | source)
XLA Modules:
  0.0 133.4 jit_solution(6644697428063162775)
XLA Ops:
  0.7 1.1 constant_dynamic-slice_fusion.2
  1.8 8.8 %collective-permute-start = (bf16[2,128,512]{2,1,0:T(8,128)(2,1)S(1)}, bf16[2,128,512]{2,1,0:T(8,128)(2,1)S(1)}, u32[]{:S(2)}, u32[]{:S(2)}) collective-permute-start(bf16[2,128,512]{2,1,0:T(8,128)(2,1)S(1)} %pad_maximum_fusion.3), channel_id=1, source_target_pairs={{0,1},{1,0},{2,3},{3,2},{4,5},{5,4},{6,7},{7,6},{8,9},{9,8},{10,11... | collective-permute-start | bytes 786440 | tf_op jit(solution)/shard_map/ppermute | solution.py:205
  10.6 1.3 dynamic-slice_bitcast_fusion
  12.1 2.0 %collective-permute-start.1 = (bf16[128,4096]{1,0:T(8,128)(2,1)S(1)}, bf16[128,4096]{1,0:T(8,128)(2,1)}, u32[]{:S(2)}, u32[]{:S(2)}) collective-permute-start(bf16[128,4096]{1,0:T(8,128)(2,1)S(1)} %pad_maximum_fusion), channel_id=1, source_target_pairs={{0,1},{1,0},{2,3},{3,2},{4,5},{5,4},{6,7},{7,6},{8,9},{9,8},{10,11... | collective-permute-start | bytes 3145736 | tf_op jit(solution)/shard_map/ppermute | solution.py:205
  14.1 1.5 %collective-permute-start.2 = (bf16[2,256,512]{2,1,0:T(8,128)(2,1)S(1)}, bf16[2,256,512]{2,1,0:T(8,128)(2,1)}, u32[]{:S(2)}, u32[]{:S(2)}) collective-permute-start(bf16[2,256,512]{2,1,0:T(8,128)(2,1)S(1)} %pad_maximum_fusion.1.own), channel_id=1, source_target_pairs={{248,254},{249,255},{250,252},{251,253},{504,510},{505,511},{506,5... | collective-permute-start | bytes 1572872 | tf_op jit(solution)/shard_map/ppermute | solution.py:214
  15.6 2.1 %collective-permute-start.5 = (bf16[2,256,512]{2,1,0:T(8,128)(2,1)S(1)}, bf16[2,256,512]{2,1,0:T(8,128)(2,1)}, u32[]{:S(2)}, u32[]{:S(2)}) collective-permute-start(bf16[2,256,512]{2,1,0:T(8,128)(2,1)S(1)} %pad_maximum_fusion.1.own), channel_id=1, source_target_pairs={{0,10},{8,18},{16,26},{24,34},{32,42},{40,50},{48,58},{56,66},{64,... | collective-permute-start | bytes 1572872 | tf_op jit(solution)/shard_map/ppermute | solution.py:217
  17.7 2.1 %collective-permute-start.4 = (bf16[2,256,512]{2,1,0:T(8,128)(2,1)S(1)}, bf16[2,256,512]{2,1,0:T(8,128)(2,1)}, u32[]{:S(2)}, u32[]{:S(2)}) collective-permute-start(bf16[2,256,512]{2,1,0:T(8,128)(2,1)S(1)} %pad_maximum_fusion.1.own), channel_id=1, source_target_pairs={{0,8},{8,16},{16,24},{24,32},{32,40},{40,48},{48,56},{56,64},{64,7... | collective-permute-start | bytes 1572872 | tf_op jit(solution)/shard_map/ppermute | solution.py:216
  19.8 2.2 %collective-permute-start.3 = (bf16[2,256,512]{2,1,0:T(8,128)(2,1)S(1)}, bf16[2,256,512]{2,1,0:T(8,128)(2,1)}, u32[]{:S(2)}, u32[]{:S(2)}) collective-permute-start(bf16[2,256,512]{2,1,0:T(8,128)(2,1)S(1)} %pad_maximum_fusion.1.own), channel_id=1, source_target_pairs={{0,2},{1,3},{4,6},{5,7},{8,10},{9,11},{12,14},{13,15},{16,18},{17,... | collective-permute-start | bytes 1572872 | tf_op jit(solution)/shard_map/ppermute | solution.py:215
  22.0 0.7 pad_add_fusion.place
  22.7 5.6 %shard_map.75.own_stats = f32[4,16,256]{2,1,0:T(8,128)} custom-call(s32[3]{0:T(128)} %pad_add_fusion.place, bf16[128,4096]{1,0:T(8,128)(2,1)} %bitcast.20, bf16[128,4096]{1,0:T(8,128)(2,1)} %collective-permute-done.1.q_theirs.g_theirs, bf16[128,4096]{1,0:T(8,128)(2,1)} %bitcast.23, bf16[128,4096]{1,0:T(8,128)(2,1)} %collective-permute-done.1.q_theirs.g_theirs, ...), custom_call_target="tpu_custom_call" | custom-call | flops 536870912 | bytes 4194304 | tf_op jit(solution)/shard_map/pallas_call | solution.py:156
  28.2 1.5 %collective-permute-start.6 = (bf16[2,256,512]{2,1,0:T(8,128)(2,1)}, bf16[2,256,512]{2,1,0:T(8,128)(2,1)}, u32[]{:S(2)}, u32[]{:S(2)}) collective-permute-start(bf16[2,256,512]{2,1,0:T(8,128)(2,1)} %collective-permute-done.2.fold_cross), channel_id=1, source_target_pairs={{252,254},{253,255},{254,252},{255,253},{508,510},{509,511},{510,5... | collective-permute-start | bytes 1572872 | tf_op jit(solution)/shard_map/ppermute | solution.py:249
  29.7 9.6 %collective-permute-done.4.same = bf16[2,256,512]{2,1,0:T(8,128)(2,1)} collective-permute-done((bf16[2,256,512]{2,1,0:T(8,128)(2,1)S(1)}, bf16[2,256,512]{2,1,0:T(8,128)(2,1)}, u32[]{:S(2)}, u32[]{:S(2)}) %collective-permute-start.4) | collective-permute-done | bytes 524320 | tf_op jit(solution)/shard_map/ppermute | solution.py:216
  39.3 16.1 %shard_map.76 = (bf16[2,256,512]{2,1,0:T(8,128)(2,1)}, bf16[2,256,512]{2,1,0:T(8,128)(2,1)}, bf16[2,256,512]{2,1,0:T(8,128)(2,1)}, bf16[4,4,768,256]{3,2,1,0:T(8,128)(2,1)}, f32[4,16,256]{2,1,0:T(8,128)}) custom-call(s32[3]{0:T(128)} %pad_add_fusion.place, bf16[128,4096]{1,0:T(8,128)(2,1)} %bitcast.21, ...), custom_call_target="tpu_custom_call" | custom-call | flops 3221225472 | bytes 4194304 | tf_op jit(solution)/shard_map/pallas_call | solution.py:156
  55.4 1.5 %collective-permute-start.11 = (bf16[2,256,512]{2,1,0:T(8,128)(2,1)}, bf16[2,256,512]{2,1,0:T(8,128)(2,1)}, u32[]{:S(2)}, u32[]{:S(2)}) collective-permute-start(bf16[2,256,512]{2,1,0:T(8,128)(2,1)} %get-tuple-element.34), channel_id=1, source_target_pairs={{254,248},{255,249},{252,250},{253,251},{510,504},{511,505},{508,5... | collective-permute-start | bytes 1572872 | tf_op jit(solution)/shard_map/ppermute | solution.py:260
  56.9 1.3 collective-permute-start.8
  58.2 1.3 collective-permute-start.9
  59.5 1.3 collective-permute-start.10
  60.8 10.8 %shard_map.77 = (bf16[128,2048]{1,0:T(8,128)(2,1)}, bf16[128,2048]{1,0:T(8,128)(2,1)}, f32[2,256,512]{2,1,0:T(8,128)}, f32[8,128]{1,0:T(8,128)}) custom-call(s32[3]{0:T(128)} %pad_add_fusion.place, bf16[128,4096]{1,0:T(8,128)(2,1)} %bitcast.22, bf16[128,4096]{1,0:T(8,128)(2,1)} %collective-permute-done.1.q_theirs.g_theirs, bf16[128,4096]{1,0:T(8,128)(2,1)} %bitcast.25, ...), custom_call_target="tpu_custom_call" | custom-call | flops 2147483648 | bytes 4194304 | tf_op jit(solution)/shard_map/pallas_call | solution.py:156
  71.6 0.7 collective-permute-start.12
  72.3 2.8 %collective-permute-start.7 = (bf16[128,2048]{1,0:T(8,128)(2,1)}, bf16[128,2048]{1,0:T(8,128)(2,1)}, u32[]{:S(2)}, u32[]{:S(2)}) collective-permute-start(bf16[128,2048]{1,0:T(8,128)(2,1)} %get-tuple-element.31), channel_id=1, source_target_pairs={{0,1},{1,0},{2,3},{3,2},{4,5},{5,4},{6,7},{7,6},{8,9},{9,8},{10,11... | collective-permute-start | bytes 1572872 | tf_op jit(solution)/shard_map/ppermute | solution.py:205
  75.2 0.7 reduce_sum.27
  75.9 1.5 %convert_add_fusion.near = f32[2,256,512]{2,1,0:T(8,128)S(1)} fusion(f32[2,256,512]{2,1,0:T(8,128)} %get-tuple-element.32, bf16[2,256,512]{2,1,0:T(8,128)(2,1)} %collective-permute-done.8), kind=kLoop, calls=%fused_computation.2 | loop fusion | flops 524288 | bytes 2621440 | tf_op jit(solution)/shard_map/add | solution.py:277
  77.4 10.2 %collective-permute-done.10.cross = bf16[2,256,512]{2,1,0:T(8,128)(2,1)} collective-permute-done((bf16[2,256,512]{2,1,0:T(8,128)(2,1)}, bf16[2,256,512]{2,1,0:T(8,128)(2,1)}, u32[]{:S(2)}, u32[]{:S(2)}) %collective-permute-start.10) | collective-permute-done | bytes 524320 | tf_op jit(solution)/shard_map/ppermute | solution.py:263
  87.6 2.3 %shard_map.78 = (bf16[2,128,512]{2,1,0:T(8,128)(2,1)S(1)}, bf16[2,128,512]{2,1,0:T(8,128)(2,1)S(1)}, f32[8,128]{1,0:T(8,128)}) custom-call(f32[2,256,512]{2,1,0:T(8,128)S(1)} %convert_add_fusion.near, bf16[2,256,512]{2,1,0:T(8,128)(2,1)S(1)} %collective-permute-done.9.same, bf16[2,256,512]{2,1,0:T(8,128)(2,1)} %collective-permute-done.10.cross, ...), custom_call_target="tpu_custom_call" | custom-call | tf_op jit(solution)/shard_map/pallas_call | solution.py:280
  89.9 5.0 %all-to-all-start = ((f32[8,1,128]{2,1,0:T(1,128)}), f32[8,1,128]{2,1,0:T(1,128)S(1)}, u32[]{:S(2)}, u32[]{:S(2)}) async-start(f32[8,1,128]{2,1,0:T(1,128)} %bitcast.10), calls=%async_computation | async-start | bytes 8192 | tf_op jit(solution)/shard_map/all_to_all | solution.py:173
  95.0 1.3 broadcast_select_fusion.1
  96.2 2.0 %collective-permute-start.13 = (bf16[2,128,512]{2,1,0:T(8,128)(2,1)S(1)}, bf16[2,128,512]{2,1,0:T(8,128)(2,1)S(1)}, u32[]{:S(2)}, u32[]{:S(2)}) collective-permute-start(bf16[2,128,512]{2,1,0:T(8,128)(2,1)S(1)} %get-tuple-element.40), channel_id=1, source_target_pairs={{0,1},{1,0},{2,3},{3,2},{4,5},{5,4},{6,7},{7,6},{8,9},{9,8},{10,11... | collective-permute-start | bytes 786440 | tf_op jit(solution)/shard_map/ppermute | solution.py:205
  98.3 1.2 all-to-all-done
  100.1 17.8 %all-to-all-start.1 = ((f32[64,1,128]{2,1,0:T(1,128)}), f32[64,1,128]{2,1,0:T(1,128)S(1)}, u32[]{:S(2)}, u32[]{:S(2)}) async-start(f32[64,1,128]{2,1,0:T(1,128)} %broadcast_in_dim.17), calls=%async_computation.1 | async-start | bytes 65536 | tf_op jit(solution)/shard_map/all_to_all | solution.py:173
  118.0 1.0 maximum_bitcast_fusion
  119.0 12.2 %all-to-all-done.1 = f32[64,1,128]{2,1,0:T(1,128)S(1)} async-done(((f32[64,1,128]{2,1,0:T(1,128)}), f32[64,1,128]{2,1,0:T(1,128)S(1)}, u32[]{:S(2)}, u32[]{:S(2)}) %all-to-all-start.1) | async-done | bytes 32800 | tf_op jit(solution)/shard_map/all_to_all | solution.py:173
  131.4 0.9 pad_maximum_fusion.2
  (21 shorter events, 0.9 us)
Async XLA Ops:
  1.8 10.2 %collective-permute-start = (bf16[2,128,512]{2,1,0:T(8,128)(2,1)S(1)}, bf16[2,128,512]{2,1,0:T(8,128)(2,1)S(1)}, u32[]{:S(2)}, u32[]{:S(2)}) collective-permute-start(bf16[2,128,512]{2,1,0:T(8,128)(2,1)S(1)} %pad_maximum_fusion.3), channel_id=1, source_target_pairs={{0,1},{1,0},{2,3},{3,2},{4,5},{5,4},{6,7},{7,6},{8,9},{9,8},{10,11... | collective-permute-start | bytes 786440 | tf_op jit(solution)/shard_map/ppermute | solution.py:205
  12.1 10.6 %copy-start = (bf16[2,256,512]{2,1,0:T(8,128)(2,1)}, bf16[2,256,512]{2,1,0:T(8,128)(2,1)S(1)}, u32[]{:S(2)}) copy-start(bf16[2,256,512]{2,1,0:T(8,128)(2,1)S(1)} %pad_maximum_fusion.1.own) | copy-start | bytes 1572868
  12.1 9.9 %collective-permute-start.1 = (bf16[128,4096]{1,0:T(8,128)(2,1)S(1)}, bf16[128,4096]{1,0:T(8,128)(2,1)}, u32[]{:S(2)}, u32[]{:S(2)}) collective-permute-start(bf16[128,4096]{1,0:T(8,128)(2,1)S(1)} %pad_maximum_fusion), channel_id=1, source_target_pairs={{0,1},{1,0},{2,3},{3,2},{4,5},{5,4},{6,7},{7,6},{8,9},{9,8},{10,11... | collective-permute-start | bytes 3145736 | tf_op jit(solution)/shard_map/ppermute | solution.py:205
  14.1 14.1 %collective-permute-start.2 = (bf16[2,256,512]{2,1,0:T(8,128)(2,1)S(1)}, bf16[2,256,512]{2,1,0:T(8,128)(2,1)}, u32[]{:S(2)}, u32[]{:S(2)}) collective-permute-start(bf16[2,256,512]{2,1,0:T(8,128)(2,1)S(1)} %pad_maximum_fusion.1.own), channel_id=1, source_target_pairs={{248,254},{249,255},{250,252},{251,253},{504,510},{505,511},{506,5... | collective-permute-start | bytes 1572872 | tf_op jit(solution)/shard_map/ppermute | solution.py:214
  15.6 14.1 %collective-permute-start.5 = (bf16[2,256,512]{2,1,0:T(8,128)(2,1)S(1)}, bf16[2,256,512]{2,1,0:T(8,128)(2,1)}, u32[]{:S(2)}, u32[]{:S(2)}) collective-permute-start(bf16[2,256,512]{2,1,0:T(8,128)(2,1)S(1)} %pad_maximum_fusion.1.own), channel_id=1, source_target_pairs={{0,10},{8,18},{16,26},{24,34},{32,42},{40,50},{48,58},{56,66},{64,... | collective-permute-start | bytes 1572872 | tf_op jit(solution)/shard_map/ppermute | solution.py:217
  17.7 21.6 %collective-permute-start.4 = (bf16[2,256,512]{2,1,0:T(8,128)(2,1)S(1)}, bf16[2,256,512]{2,1,0:T(8,128)(2,1)}, u32[]{:S(2)}, u32[]{:S(2)}) collective-permute-start(bf16[2,256,512]{2,1,0:T(8,128)(2,1)S(1)} %pad_maximum_fusion.1.own), channel_id=1, source_target_pairs={{0,8},{8,16},{16,24},{24,32},{32,40},{40,48},{48,56},{56,64},{64,7... | collective-permute-start | bytes 1572872 | tf_op jit(solution)/shard_map/ppermute | solution.py:216
  19.8 19.5 %collective-permute-start.3 = (bf16[2,256,512]{2,1,0:T(8,128)(2,1)S(1)}, bf16[2,256,512]{2,1,0:T(8,128)(2,1)}, u32[]{:S(2)}, u32[]{:S(2)}) collective-permute-start(bf16[2,256,512]{2,1,0:T(8,128)(2,1)S(1)} %pad_maximum_fusion.1.own), channel_id=1, source_target_pairs={{0,2},{1,3},{4,6},{5,7},{8,10},{9,11},{12,14},{13,15},{16,18},{17,... | collective-permute-start | bytes 1572872 | tf_op jit(solution)/shard_map/ppermute | solution.py:215
  28.2 11.1 %collective-permute-start.6 = (bf16[2,256,512]{2,1,0:T(8,128)(2,1)}, bf16[2,256,512]{2,1,0:T(8,128)(2,1)}, u32[]{:S(2)}, u32[]{:S(2)}) collective-permute-start(bf16[2,256,512]{2,1,0:T(8,128)(2,1)} %collective-permute-done.2.fold_cross), channel_id=1, source_target_pairs={{252,254},{253,255},{254,252},{255,253},{508,510},{509,511},{510,5... | collective-permute-start | bytes 1572872 | tf_op jit(solution)/shard_map/ppermute | solution.py:249
  55.4 16.2 %collective-permute-start.11 = (bf16[2,256,512]{2,1,0:T(8,128)(2,1)}, bf16[2,256,512]{2,1,0:T(8,128)(2,1)}, u32[]{:S(2)}, u32[]{:S(2)}) collective-permute-start(bf16[2,256,512]{2,1,0:T(8,128)(2,1)} %get-tuple-element.34), channel_id=1, source_target_pairs={{254,248},{255,249},{252,250},{253,251},{510,504},{511,505},{508,5... | collective-permute-start | bytes 1572872 | tf_op jit(solution)/shard_map/ppermute | solution.py:260
  56.9 18.9 %collective-permute-start.8 = (bf16[2,256,512]{2,1,0:T(8,128)(2,1)}, bf16[2,256,512]{2,1,0:T(8,128)(2,1)}, u32[]{:S(2)}, u32[]{:S(2)}) collective-permute-start(bf16[2,256,512]{2,1,0:T(8,128)(2,1)} %get-tuple-element.33), channel_id=1, source_target_pairs={{2,0},{3,1},{6,4},{7,5},{10,8},{11,9},{14,12},{15,13},{18,16},{19,... | collective-permute-start | bytes 1572872 | tf_op jit(solution)/shard_map/ppermute | solution.py:261
  58.2 29.4 %collective-permute-start.9 = (bf16[2,256,512]{2,1,0:T(8,128)(2,1)}, bf16[2,256,512]{2,1,0:T(8,128)(2,1)S(1)}, u32[]{:S(2)}, u32[]{:S(2)}) collective-permute-start(bf16[2,256,512]{2,1,0:T(8,128)(2,1)} %get-tuple-element.34), channel_id=1, source_target_pairs={{8,0},{16,8},{24,16},{32,24},{40,32},{48,40},{56,48},{64,56},{72,6... | collective-permute-start | bytes 1572872 | tf_op jit(solution)/shard_map/ppermute | solution.py:262
  59.5 28.1 %collective-permute-start.10 = (bf16[2,256,512]{2,1,0:T(8,128)(2,1)}, bf16[2,256,512]{2,1,0:T(8,128)(2,1)}, u32[]{:S(2)}, u32[]{:S(2)}) collective-permute-start(bf16[2,256,512]{2,1,0:T(8,128)(2,1)} %get-tuple-element.35), channel_id=1, source_target_pairs={{10,0},{18,8},{26,16},{34,24},{42,32},{50,40},{58,48},{66,56},{74,... | collective-permute-start | bytes 1572872 | tf_op jit(solution)/shard_map/ppermute | solution.py:263
  71.6 16.0 %collective-permute-start.12 = (bf16[2,256,512]{2,1,0:T(8,128)(2,1)}, bf16[2,256,512]{2,1,0:T(8,128)(2,1)S(1)}, u32[]{:S(2)}, u32[]{:S(2)}) collective-permute-start(bf16[2,256,512]{2,1,0:T(8,128)(2,1)} %collective-permute-done.11), channel_id=1, source_target_pairs={{248,250},{249,251},{250,248},{251,249},{504,506},{505,507},{506,5... | collective-permute-start | bytes 1572872 | tf_op jit(solution)/shard_map/ppermute | solution.py:275
  72.3 22.6 %collective-permute-start.7 = (bf16[128,2048]{1,0:T(8,128)(2,1)}, bf16[128,2048]{1,0:T(8,128)(2,1)}, u32[]{:S(2)}, u32[]{:S(2)}) collective-permute-start(bf16[128,2048]{1,0:T(8,128)(2,1)} %get-tuple-element.31), channel_id=1, source_target_pairs={{0,1},{1,0},{2,3},{3,2},{4,5},{5,4},{6,7},{7,6},{8,9},{9,8},{10,11... | collective-permute-start | bytes 1572872 | tf_op jit(solution)/shard_map/ppermute | solution.py:205
  89.9 9.6 %all-to-all-start = ((f32[8,1,128]{2,1,0:T(1,128)}), f32[8,1,128]{2,1,0:T(1,128)S(1)}, u32[]{:S(2)}, u32[]{:S(2)}) async-start(f32[8,1,128]{2,1,0:T(1,128)} %bitcast.10), calls=%async_computation | async-start | bytes 8192 | tf_op jit(solution)/shard_map/all_to_all | solution.py:173
  96.2 35.1 %collective-permute-start.13 = (bf16[2,128,512]{2,1,0:T(8,128)(2,1)S(1)}, bf16[2,128,512]{2,1,0:T(8,128)(2,1)S(1)}, u32[]{:S(2)}, u32[]{:S(2)}) collective-permute-start(bf16[2,128,512]{2,1,0:T(8,128)(2,1)S(1)} %get-tuple-element.40), channel_id=1, source_target_pairs={{0,1},{1,0},{2,3},{3,2},{4,5},{5,4},{6,7},{7,6},{8,9},{9,8},{10,11... | collective-permute-start | bytes 786440 | tf_op jit(solution)/shard_map/ppermute | solution.py:205
  100.1 31.1 %all-to-all-start.1 = ((f32[64,1,128]{2,1,0:T(1,128)}), f32[64,1,128]{2,1,0:T(1,128)S(1)}, u32[]{:S(2)}, u32[]{:S(2)}) async-start(f32[64,1,128]{2,1,0:T(1,128)} %broadcast_in_dim.17), calls=%async_computation.1 | async-start | bytes 65536 | tf_op jit(solution)/shard_map/all_to_all | solution.py:173

commit v5 on v4

--- a/solution.py
+++ b/solution.py
@@ -152,7 +152,7 @@
     sums[...] = jnp.broadcast_to(square, sums.shape)
 
 
-def call(kernel, groups, ins, outs, flops, exps, *args):
+def call(kernel, groups, ins, outs, flops, exps, *args, grant=VMEM):
     return pl.pallas_call(
         kernel,
         grid_spec=pltpu.PrefetchScalarGridSpec(
@@ -162,7 +162,7 @@
             out_specs=[spec for spec, _ in outs],
         ),
         out_shape=[shape for _, shape in outs],
-        compiler_params=pltpu.CompilerParams(vmem_limit_bytes=VMEM),
+        compiler_params=pltpu.CompilerParams(vmem_limit_bytes=grant),
         cost_estimate=pl.CostEstimate(
             flops=flops, bytes_accessed=4 * 1024 * 1024, transcendentals=exps
         ),
@@ -269,7 +269,7 @@
         + [(square_spec, jax.ShapeDtypeStruct((8, HEAD_SIZE), jnp.float32))],
         8 * unit,
         exps,
-        *rows_in, stats, own, side, same, cross, fold_same, fold_cross, dscores,
+        *rows_in, stats, own, side, same, cross, fold_same, fold_cross, dscores, grant=60 * 1024 * 1024,
     )
     fold_grad, dq_squares = lax.optimization_barrier((fold_grad, dq_squares))
     from_fold = lax.ppermute(fold_grad, both, fold_near_back)

time: 134 us -> 132 us (0.985)
  transfers between devices with their start and end apart: 16 -> 16, of which waited for: 4 -> 4; matrix products, arithmetic and copies ran while one was open for 5% -> 5% of each run, Pallas kernels for 14% -> 13%
where the time goes in v5:
time: 132 us; the launch traced here: 131 us
  starting transfers between devices  54 us (41%)
  waiting for transfers between devices  33.7 us (26%)
  Pallas kernels  33.7 us (26%)
  other arithmetic  4.96 us (4%)
  local copies, waits for them, and re-layouts  3.08 us (2%)
  between operations  2.08 us (2%)
    pallas_call x3, Pallas kernels, call(): pl.pallas_call(kernel, grid_spec=pltpu.PrefetchScalarGridSpec(num_scalar_...  32.4 us
    all_to_all x2, starting transfers between devices, all_sum(): given = lax.all_to_all(x, axes, 0, 0, tiled=True)  22.9 us
    ppermute x4, starting transfers between devices, swap_core(): return lax.ppermute(x, 'head', core_pairs)  15.7 us
    all_to_all x2, waiting for transfers between devices, all_sum(): given = lax.all_to_all(x, axes, 0, 0, tiled=True)  14.6 us
    ppermute x1, waiting for transfers between devices, body(): same = lax.ppermute(own, both, chain)  9.63 us
    ppermute x1, waiting for transfers between devices, body(): next_cross = lax.ppermute(cross_grad, both, slant_back)  9.39 us
  transfers between devices with their start and end apart: 16, of which 4 were waited for; matrix products, arithmetic and copies ran while one was open for 5% of the time, Pallas kernels for 13%

profile of v5, /device:TPU:1, one launch (start us, length us, event | category | flops | bytes accessed | tf_op | source)
XLA Modules:
  0.0 131.4 jit_solution(16764577852904896435)
XLA Ops:
  0.7 1.1 constant_dynamic-slice_fusion.2
  1.8 8.8 %collective-permute-start = (bf16[2,128,512]{2,1,0:T(8,128)(2,1)S(1)}, bf16[2,128,512]{2,1,0:T(8,128)(2,1)S(1)}, u32[]{:S(2)}, u32[]{:S(2)}) collective-permute-start(bf16[2,128,512]{2,1,0:T(8,128)(2,1)S(1)} %pad_maximum_fusion.3), channel_id=1, source_target_pairs={{0,1},{1,0},{2,3},{3,2},{4,5},{5,4},{6,7},{7,6},{8,9},{9,8},{10,11... | collective-permute-start | bytes 786440 | tf_op jit(solution)/shard_map/ppermute | solution.py:205
  10.6 1.3 dynamic-slice_bitcast_fusion
  12.1 2.0 %collective-permute-start.1 = (bf16[128,4096]{1,0:T(8,128)(2,1)S(1)}, bf16[128,4096]{1,0:T(8,128)(2,1)}, u32[]{:S(2)}, u32[]{:S(2)}) collective-permute-start(bf16[128,4096]{1,0:T(8,128)(2,1)S(1)} %pad_maximum_fusion), channel_id=1, source_target_pairs={{0,1},{1,0},{2,3},{3,2},{4,5},{5,4},{6,7},{7,6},{8,9},{9,8},{10,11... | collective-permute-start | bytes 3145736 | tf_op jit(solution)/shard_map/ppermute | solution.py:205
  14.1 1.5 %collective-permute-start.2 = (bf16[2,256,512]{2,1,0:T(8,128)(2,1)S(1)}, bf16[2,256,512]{2,1,0:T(8,128)(2,1)}, u32[]{:S(2)}, u32[]{:S(2)}) collective-permute-start(bf16[2,256,512]{2,1,0:T(8,128)(2,1)S(1)} %pad_maximum_fusion.1.own), channel_id=1, source_target_pairs={{248,254},{249,255},{250,252},{251,253},{504,510},{505,511},{506,5... | collective-permute-start | bytes 1572872 | tf_op jit(solution)/shard_map/ppermute | solution.py:214
  15.6 2.1 %collective-permute-start.5 = (bf16[2,256,512]{2,1,0:T(8,128)(2,1)S(1)}, bf16[2,256,512]{2,1,0:T(8,128)(2,1)}, u32[]{:S(2)}, u32[]{:S(2)}) collective-permute-start(bf16[2,256,512]{2,1,0:T(8,128)(2,1)S(1)} %pad_maximum_fusion.1.own), channel_id=1, source_target_pairs={{0,10},{8,18},{16,26},{24,34},{32,42},{40,50},{48,58},{56,66},{64,... | collective-permute-start | bytes 1572872 | tf_op jit(solution)/shard_map/ppermute | solution.py:217
  17.7 2.1 %collective-permute-start.4 = (bf16[2,256,512]{2,1,0:T(8,128)(2,1)S(1)}, bf16[2,256,512]{2,1,0:T(8,128)(2,1)}, u32[]{:S(2)}, u32[]{:S(2)}) collective-permute-start(bf16[2,256,512]{2,1,0:T(8,128)(2,1)S(1)} %pad_maximum_fusion.1.own), channel_id=1, source_target_pairs={{0,8},{8,16},{16,24},{24,32},{32,40},{40,48},{48,56},{56,64},{64,7... | collective-permute-start | bytes 1572872 | tf_op jit(solution)/shard_map/ppermute | solution.py:216
  19.8 2.2 %collective-permute-start.3 = (bf16[2,256,512]{2,1,0:T(8,128)(2,1)S(1)}, bf16[2,256,512]{2,1,0:T(8,128)(2,1)}, u32[]{:S(2)}, u32[]{:S(2)}) collective-permute-start(bf16[2,256,512]{2,1,0:T(8,128)(2,1)S(1)} %pad_maximum_fusion.1.own), channel_id=1, source_target_pairs={{0,2},{1,3},{4,6},{5,7},{8,10},{9,11},{12,14},{13,15},{16,18},{17,... | collective-permute-start | bytes 1572872 | tf_op jit(solution)/shard_map/ppermute | solution.py:215
  22.1 0.6 pad_add_fusion.place
  22.7 5.6 %shard_map.75.own_stats = f32[4,16,256]{2,1,0:T(8,128)} custom-call(s32[3]{0:T(128)} %pad_add_fusion.place, bf16[128,4096]{1,0:T(8,128)(2,1)} %bitcast.20, bf16[128,4096]{1,0:T(8,128)(2,1)} %collective-permute-done.1.q_theirs.g_theirs, bf16[128,4096]{1,0:T(8,128)(2,1)} %bitcast.23, bf16[128,4096]{1,0:T(8,128)(2,1)} %collective-permute-done.1.q_theirs.g_theirs, ...), custom_call_target="tpu_custom_call" | custom-call | flops 536870912 | bytes 4194304 | tf_op jit(solution)/shard_map/pallas_call | solution.py:156
  28.2 1.5 %collective-permute-start.6 = (bf16[2,256,512]{2,1,0:T(8,128)(2,1)}, bf16[2,256,512]{2,1,0:T(8,128)(2,1)}, u32[]{:S(2)}, u32[]{:S(2)}) collective-permute-start(bf16[2,256,512]{2,1,0:T(8,128)(2,1)} %collective-permute-done.2.fold_cross), channel_id=1, source_target_pairs={{252,254},{253,255},{254,252},{255,253},{508,510},{509,511},{510,5... | collective-permute-start | bytes 1572872 | tf_op jit(solution)/shard_map/ppermute | solution.py:249
  29.7 9.6 %collective-permute-done.4.same = bf16[2,256,512]{2,1,0:T(8,128)(2,1)} collective-permute-done((bf16[2,256,512]{2,1,0:T(8,128)(2,1)S(1)}, bf16[2,256,512]{2,1,0:T(8,128)(2,1)}, u32[]{:S(2)}, u32[]{:S(2)}) %collective-permute-start.4) | collective-permute-done | bytes 524320 | tf_op jit(solution)/shard_map/ppermute | solution.py:216
  39.3 16.1 %shard_map.76 = (bf16[2,256,512]{2,1,0:T(8,128)(2,1)}, bf16[2,256,512]{2,1,0:T(8,128)(2,1)}, bf16[2,256,512]{2,1,0:T(8,128)(2,1)}, bf16[4,4,768,256]{3,2,1,0:T(8,128)(2,1)}, f32[4,16,256]{2,1,0:T(8,128)}) custom-call(s32[3]{0:T(128)} %pad_add_fusion.place, bf16[128,4096]{1,0:T(8,128)(2,1)} %bitcast.21, ...), custom_call_target="tpu_custom_call" | custom-call | flops 3221225472 | bytes 4194304 | tf_op jit(solution)/shard_map/pallas_call | solution.py:156
  55.4 1.5 %collective-permute-start.11 = (bf16[2,256,512]{2,1,0:T(8,128)(2,1)}, bf16[2,256,512]{2,1,0:T(8,128)(2,1)}, u32[]{:S(2)}, u32[]{:S(2)}) collective-permute-start(bf16[2,256,512]{2,1,0:T(8,128)(2,1)} %get-tuple-element.34), channel_id=1, source_target_pairs={{254,248},{255,249},{252,250},{253,251},{510,504},{511,505},{508,5... | collective-permute-start | bytes 1572872 | tf_op jit(solution)/shard_map/ppermute | solution.py:260
  56.9 1.3 collective-permute-start.8
  58.2 1.3 collective-permute-start.9
  59.5 1.3 collective-permute-start.10
  60.8 10.8 %shard_map.77 = (bf16[128,2048]{1,0:T(8,128)(2,1)}, bf16[128,2048]{1,0:T(8,128)(2,1)}, f32[2,256,512]{2,1,0:T(8,128)}, f32[8,128]{1,0:T(8,128)}) custom-call(s32[3]{0:T(128)} %pad_add_fusion.place, bf16[128,4096]{1,0:T(8,128)(2,1)} %bitcast.22, bf16[128,4096]{1,0:T(8,128)(2,1)} %collective-permute-done.1.q_theirs.g_theirs, bf16[128,4096]{1,0:T(8,128)(2,1)} %bitcast.25, ...), custom_call_target="tpu_custom_call" | custom-call | flops 2147483648 | bytes 4194304 | tf_op jit(solution)/shard_map/pallas_call | solution.py:156
  71.6 0.7 collective-permute-start.12
  72.3 2.8 %collective-permute-start.7 = (bf16[128,2048]{1,0:T(8,128)(2,1)}, bf16[128,2048]{1,0:T(8,128)(2,1)S(1)}, u32[]{:S(2)}, u32[]{:S(2)}) collective-permute-start(bf16[128,2048]{1,0:T(8,128)(2,1)} %get-tuple-element.31), channel_id=1, source_target_pairs={{0,1},{1,0},{2,3},{3,2},{4,5},{5,4},{6,7},{7,6},{8,9},{9,8},{10,11... | collective-permute-start | bytes 1572872 | tf_op jit(solution)/shard_map/ppermute | solution.py:205
  75.1 0.7 reduce_sum.27
  75.8 1.5 %convert_add_fusion.near = f32[2,256,512]{2,1,0:T(8,128)S(1)} fusion(f32[2,256,512]{2,1,0:T(8,128)} %get-tuple-element.32, bf16[2,256,512]{2,1,0:T(8,128)(2,1)S(1)} %collective-permute-done.8), kind=kLoop, calls=%fused_computation.2 | loop fusion | flops 524288 | bytes 2621440 | tf_op jit(solution)/shard_map/add | solution.py:277
  77.3 9.4 %collective-permute-done.10.cross = bf16[2,256,512]{2,1,0:T(8,128)(2,1)S(1)} collective-permute-done((bf16[2,256,512]{2,1,0:T(8,128)(2,1)}, bf16[2,256,512]{2,1,0:T(8,128)(2,1)S(1)}, u32[]{:S(2)}, u32[]{:S(2)}) %collective-permute-start.10) | collective-permute-done | bytes 524320 | tf_op jit(solution)/shard_map/ppermute | solution.py:263
  86.7 1.2 shard_map.78
  87.9 5.0 %all-to-all-start = ((f32[8,1,128]{2,1,0:T(1,128)}), f32[8,1,128]{2,1,0:T(1,128)S(1)}, u32[]{:S(2)}, u32[]{:S(2)}) async-start(f32[8,1,128]{2,1,0:T(1,128)} %bitcast.10), calls=%async_computation | async-start | bytes 8192 | tf_op jit(solution)/shard_map/all_to_all | solution.py:173
  93.1 2.0 %collective-permute-start.13 = (bf16[2,128,512]{2,1,0:T(8,128)(2,1)S(1)}, bf16[2,128,512]{2,1,0:T(8,128)(2,1)S(1)}, u32[]{:S(2)}, u32[]{:S(2)}) collective-permute-start(bf16[2,128,512]{2,1,0:T(8,128)(2,1)S(1)} %get-tuple-element.40), channel_id=1, source_target_pairs={{0,1},{1,0},{2,3},{3,2},{4,5},{5,4},{6,7},{7,6},{8,9},{9,8},{10,11... | collective-permute-start | bytes 786440 | tf_op jit(solution)/shard_map/ppermute | solution.py:205
  95.1 2.4 %all-to-all-done = f32[8,1,128]{2,1,0:T(1,128)S(1)} async-done(((f32[8,1,128]{2,1,0:T(1,128)}), f32[8,1,128]{2,1,0:T(1,128)S(1)}, u32[]{:S(2)}, u32[]{:S(2)}) %all-to-all-start) | async-done | bytes 4128 | tf_op jit(solution)/shard_map/all_to_all | solution.py:173
  97.5 0.6 broadcast_in_dim.17
  98.2 17.8 %all-to-all-start.1 = ((f32[64,1,128]{2,1,0:T(1,128)}), f32[64,1,128]{2,1,0:T(1,128)S(1)}, u32[]{:S(2)}, u32[]{:S(2)}) async-start(f32[64,1,128]{2,1,0:T(1,128)} %broadcast_in_dim.17), calls=%async_computation.1 | async-start | bytes 65536 | tf_op jit(solution)/shard_map/all_to_all | solution.py:173
  116.0 1.0 maximum_bitcast_fusion
  117.0 12.2 %all-to-all-done.1 = f32[64,1,128]{2,1,0:T(1,128)S(1)} async-done(((f32[64,1,128]{2,1,0:T(1,128)}), f32[64,1,128]{2,1,0:T(1,128)S(1)}, u32[]{:S(2)}, u32[]{:S(2)}) %all-to-all-start.1) | async-done | bytes 32800 | tf_op jit(solution)/shard_map/all_to_all | solution.py:173
  129.4 0.8 pad_maximum_fusion.2
  (23 shorter events, 0.3 us)
Async XLA Ops:
  1.8 10.2 %collective-permute-start = (bf16[2,128,512]{2,1,0:T(8,128)(2,1)S(1)}, bf16[2,128,512]{2,1,0:T(8,128)(2,1)S(1)}, u32[]{:S(2)}, u32[]{:S(2)}) collective-permute-start(bf16[2,128,512]{2,1,0:T(8,128)(2,1)S(1)} %pad_maximum_fusion.3), channel_id=1, source_target_pairs={{0,1},{1,0},{2,3},{3,2},{4,5},{5,4},{6,7},{7,6},{8,9},{9,8},{10,11... | collective-permute-start | bytes 786440 | tf_op jit(solution)/shard_map/ppermute | solution.py:205
  12.1 10.6 %copy-start = (bf16[2,256,512]{2,1,0:T(8,128)(2,1)}, bf16[2,256,512]{2,1,0:T(8,128)(2,1)S(1)}, u32[]{:S(2)}) copy-start(bf16[2,256,512]{2,1,0:T(8,128)(2,1)S(1)} %pad_maximum_fusion.1.own) | copy-start | bytes 1572868
  12.1 10.0 %collective-permute-start.1 = (bf16[128,4096]{1,0:T(8,128)(2,1)S(1)}, bf16[128,4096]{1,0:T(8,128)(2,1)}, u32[]{:S(2)}, u32[]{:S(2)}) collective-permute-start(bf16[128,4096]{1,0:T(8,128)(2,1)S(1)} %pad_maximum_fusion), channel_id=1, source_target_pairs={{0,1},{1,0},{2,3},{3,2},{4,5},{5,4},{6,7},{7,6},{8,9},{9,8},{10,11... | collective-permute-start | bytes 3145736 | tf_op jit(solution)/shard_map/ppermute | solution.py:205
  14.1 14.1 %collective-permute-start.2 = (bf16[2,256,512]{2,1,0:T(8,128)(2,1)S(1)}, bf16[2,256,512]{2,1,0:T(8,128)(2,1)}, u32[]{:S(2)}, u32[]{:S(2)}) collective-permute-start(bf16[2,256,512]{2,1,0:T(8,128)(2,1)S(1)} %pad_maximum_fusion.1.own), channel_id=1, source_target_pairs={{248,254},{249,255},{250,252},{251,253},{504,510},{505,511},{506,5... | collective-permute-start | bytes 1572872 | tf_op jit(solution)/shard_map/ppermute | solution.py:214
  15.6 14.1 %collective-permute-start.5 = (bf16[2,256,512]{2,1,0:T(8,128)(2,1)S(1)}, bf16[2,256,512]{2,1,0:T(8,128)(2,1)}, u32[]{:S(2)}, u32[]{:S(2)}) collective-permute-start(bf16[2,256,512]{2,1,0:T(8,128)(2,1)S(1)} %pad_maximum_fusion.1.own), channel_id=1, source_target_pairs={{0,10},{8,18},{16,26},{24,34},{32,42},{40,50},{48,58},{56,66},{64,... | collective-permute-start | bytes 1572872 | tf_op jit(solution)/shard_map/ppermute | solution.py:217
  17.7 21.7 %collective-permute-start.4 = (bf16[2,256,512]{2,1,0:T(8,128)(2,1)S(1)}, bf16[2,256,512]{2,1,0:T(8,128)(2,1)}, u32[]{:S(2)}, u32[]{:S(2)}) collective-permute-start(bf16[2,256,512]{2,1,0:T(8,128)(2,1)S(1)} %pad_maximum_fusion.1.own), channel_id=1, source_target_pairs={{0,8},{8,16},{16,24},{24,32},{32,40},{40,48},{48,56},{56,64},{64,7... | collective-permute-start | bytes 1572872 | tf_op jit(solution)/shard_map/ppermute | solution.py:216
  19.8 19.5 %collective-permute-start.3 = (bf16[2,256,512]{2,1,0:T(8,128)(2,1)S(1)}, bf16[2,256,512]{2,1,0:T(8,128)(2,1)}, u32[]{:S(2)}, u32[]{:S(2)}) collective-permute-start(bf16[2,256,512]{2,1,0:T(8,128)(2,1)S(1)} %pad_maximum_fusion.1.own), channel_id=1, source_target_pairs={{0,2},{1,3},{4,6},{5,7},{8,10},{9,11},{12,14},{13,15},{16,18},{17,... | collective-permute-start | bytes 1572872 | tf_op jit(solution)/shard_map/ppermute | solution.py:215
  28.2 11.1 %collective-permute-start.6 = (bf16[2,256,512]{2,1,0:T(8,128)(2,1)}, bf16[2,256,512]{2,1,0:T(8,128)(2,1)}, u32[]{:S(2)}, u32[]{:S(2)}) collective-permute-start(bf16[2,256,512]{2,1,0:T(8,128)(2,1)} %collective-permute-done.2.fold_cross), channel_id=1, source_target_pairs={{252,254},{253,255},{254,252},{255,253},{508,510},{509,511},{510,5... | collective-permute-start | bytes 1572872 | tf_op jit(solution)/shard_map/ppermute | solution.py:249
  55.4 16.2 %collective-permute-start.11 = (bf16[2,256,512]{2,1,0:T(8,128)(2,1)}, bf16[2,256,512]{2,1,0:T(8,128)(2,1)}, u32[]{:S(2)}, u32[]{:S(2)}) collective-permute-start(bf16[2,256,512]{2,1,0:T(8,128)(2,1)} %get-tuple-element.34), channel_id=1, source_target_pairs={{254,248},{255,249},{252,250},{253,251},{510,504},{511,505},{508,5... | collective-permute-start | bytes 1572872 | tf_op jit(solution)/shard_map/ppermute | solution.py:260
  56.9 19.0 %collective-permute-start.8 = (bf16[2,256,512]{2,1,0:T(8,128)(2,1)}, bf16[2,256,512]{2,1,0:T(8,128)(2,1)S(1)}, u32[]{:S(2)}, u32[]{:S(2)}) collective-permute-start(bf16[2,256,512]{2,1,0:T(8,128)(2,1)} %get-tuple-element.33), channel_id=1, source_target_pairs={{2,0},{3,1},{6,4},{7,5},{10,8},{11,9},{14,12},{15,13},{18,16},{19,... | collective-permute-start | bytes 1572872 | tf_op jit(solution)/shard_map/ppermute | solution.py:261
  58.2 28.5 %collective-permute-start.9 = (bf16[2,256,512]{2,1,0:T(8,128)(2,1)}, bf16[2,256,512]{2,1,0:T(8,128)(2,1)S(1)}, u32[]{:S(2)}, u32[]{:S(2)}) collective-permute-start(bf16[2,256,512]{2,1,0:T(8,128)(2,1)} %get-tuple-element.34), channel_id=1, source_target_pairs={{8,0},{16,8},{24,16},{32,24},{40,32},{48,40},{56,48},{64,56},{72,6... | collective-permute-start | bytes 1572872 | tf_op jit(solution)/shard_map/ppermute | solution.py:262
  59.5 27.2 %collective-permute-start.10 = (bf16[2,256,512]{2,1,0:T(8,128)(2,1)}, bf16[2,256,512]{2,1,0:T(8,128)(2,1)S(1)}, u32[]{:S(2)}, u32[]{:S(2)}) collective-permute-start(bf16[2,256,512]{2,1,0:T(8,128)(2,1)} %get-tuple-element.35), channel_id=1, source_target_pairs={{10,0},{18,8},{26,16},{34,24},{42,32},{50,40},{58,48},{66,56},{74,... | collective-permute-start | bytes 1572872 | tf_op jit(solution)/shard_map/ppermute | solution.py:263
  71.6 15.1 %collective-permute-start.12 = (bf16[2,256,512]{2,1,0:T(8,128)(2,1)}, bf16[2,256,512]{2,1,0:T(8,128)(2,1)S(1)}, u32[]{:S(2)}, u32[]{:S(2)}) collective-permute-start(bf16[2,256,512]{2,1,0:T(8,128)(2,1)} %collective-permute-done.11), channel_id=1, source_target_pairs={{248,250},{249,251},{250,248},{251,249},{504,506},{505,507},{506,5... | collective-permute-start | bytes 1572872 | tf_op jit(solution)/shard_map/ppermute | solution.py:275
  72.3 20.7 %collective-permute-start.7 = (bf16[128,2048]{1,0:T(8,128)(2,1)}, bf16[128,2048]{1,0:T(8,128)(2,1)S(1)}, u32[]{:S(2)}, u32[]{:S(2)}) collective-permute-start(bf16[128,2048]{1,0:T(8,128)(2,1)} %get-tuple-element.31), channel_id=1, source_target_pairs={{0,1},{1,0},{2,3},{3,2},{4,5},{5,4},{6,7},{7,6},{8,9},{9,8},{10,11... | collective-permute-start | bytes 1572872 | tf_op jit(solution)/shard_map/ppermute | solution.py:205
  75.8 17.2 %copy-start.1 = (bf16[128,2048]{1,0:T(8,128)(2,1)S(1)}, bf16[128,2048]{1,0:T(8,128)(2,1)}, u32[]{:S(2)}) copy-start(bf16[128,2048]{1,0:T(8,128)(2,1)} %get-tuple-element.30) | copy-start | bytes 1572868
  87.9 9.6 %all-to-all-start = ((f32[8,1,128]{2,1,0:T(1,128)}), f32[8,1,128]{2,1,0:T(1,128)S(1)}, u32[]{:S(2)}, u32[]{:S(2)}) async-start(f32[8,1,128]{2,1,0:T(1,128)} %bitcast.10), calls=%async_computation | async-start | bytes 8192 | tf_op jit(solution)/shard_map/all_to_all | solution.py:173
  93.1 36.3 %collective-permute-start.13 = (bf16[2,128,512]{2,1,0:T(8,128)(2,1)S(1)}, bf16[2,128,512]{2,1,0:T(8,128)(2,1)S(1)}, u32[]{:S(2)}, u32[]{:S(2)}) collective-permute-start(bf16[2,128,512]{2,1,0:T(8,128)(2,1)S(1)} %get-tuple-element.40), channel_id=1, source_target_pairs={{0,1},{1,0},{2,3},{3,2},{4,5},{5,4},{6,7},{7,6},{8,9},{9,8},{10,11... | collective-permute-start | bytes 786440 | tf_op jit(solution)/shard_map/ppermute | solution.py:205
  98.2 31.1 %all-to-all-start.1 = ((f32[64,1,128]{2,1,0:T(1,128)}), f32[64,1,128]{2,1,0:T(1,128)S(1)}, u32[]{:S(2)}, u32[]{:S(2)}) async-start(f32[64,1,128]{2,1,0:T(1,128)} %broadcast_in_dim.17), calls=%async_computation.1 | async-start | bytes 65536 | tf_op jit(solution)/shard_map/all_to_all | solution.py:173
